TPU v7x, 128 devices: a whole 4x4x4 slice. The times are simulated.
128 devices in a mesh: wide: 8 (over z, core), narrow: 16 (over x, y).
Axes of the slice: x: 4, y: 4, z: 4, core: 2. Of those that a mesh axis runs over, the one named last changes fastest.
Arguments:
- feat_a: bfloat16 [8, 16, 2048, 512], P('wide', 'narrow')
- feat_b: bfloat16 [8, 16, 2048, 512], P('wide', 'narrow')
- w_hidden: bfloat16 [512, 512], replicated, may hold values from -0.25 to 0.25
- w_out: bfloat16 [512, 256], replicated, may hold values from -0.25 to 0.25
- send_rows: int32 [8, 16, 16, 128], P('wide', 'narrow'), may hold values from 0 to 2047, as said below
- dest_rows: int32 [8, 16, 16, 128], P('wide', 'narrow'), may hold values from 0 to 2047, as said below
- counts: int32 [8, 16, 16], P('wide', 'narrow'), may hold values from 16 to 128, as said below
- neg_rows: int32 [8, 16, 128], P('wide', 'narrow'), may hold values from 0 to 2047
Outputs:
- loss: float32 [], replicated
- grad_feat_a: bfloat16 [8, 16, 2048, 512], P('wide', 'narrow')
- grad_feat_b: bfloat16 [8, 16, 2048, 512], P('wide', 'narrow')
- grad_w_hidden: float32 [512, 512], replicated
- grad_w_out: float32 [512, 256], replicated
Inputs may be any that keep to these rules, and one draw needn't show every extreme that they name: `counts`: in every draw some destination gets all 128 slots live from every source of its group, and some source fills all 128 slots for every destination. `send_rows`: on each device every view-B row stands in exactly one of its slots to the destinations. `dest_rows`: on each destination every view-A row is named by exactly one of the slots arriving from the sources of its group.
All inputs are finite; a program needn't handle non-finite values.
Results may differ from a plain program's by a relative error of at most 0.04.
Values may be sent and summed in bfloat16 or wider, within the bound.
A program may use at most 128 MiB of HBM per device.

v0:
```python
import jax
import jax.numpy as jnp
from jax import lax
from jax.sharding import PartitionSpec as P

sharpness_divisor = 0.07


def finish(linear, sum_lin, square_lin, all_points, w_out):
    mean_lin = sum_lin / all_points
    var_lin = square_lin / all_points - mean_lin * mean_lin
    inv_std = lax.rsqrt(var_lin + 1e-05)
    normed = (linear - mean_lin) * inv_std
    active = jnp.maximum(normed, 0.0).astype(jnp.bfloat16)
    out_rows = jnp.dot(active, w_out, preferred_element_type=jnp.float32)
    unit_scale = lax.rsqrt(jnp.sum(out_rows * out_rows, axis=1, keepdims=True) + 1e-06)
    return (normed, inv_std, active, unit_scale, out_rows * unit_scale)


def pair_terms(
    probe_entry_count,
    key_rows,
    usable_pair_indicator,
    contrast_sample_entries,
    parameter_derivative,
):
    probe_embedding_matrix = probe_entry_count.astype(jnp.float32)
    anchor_embedding_matrix = key_rows.astype(jnp.float32)
    matched_similarity_score = (
        jnp.sum(probe_embedding_matrix * anchor_embedding_matrix, axis=1) / sharpness_divisor
    )
    compared_entry_count = (
        lax.dot_general(
            probe_entry_count,
            contrast_sample_entries,
            (((1,), (1,)), ((), ())),
            preferred_element_type=jnp.float32,
        )
        / sharpness_divisor
    )
    exp_pos = jnp.exp(matched_similarity_score)
    exp_neg = jnp.exp(compared_entry_count)
    denominator = exp_pos + jnp.sum(exp_neg, axis=1)
    loss_sum = jnp.sum((jnp.log(denominator) - matched_similarity_score) * usable_pair_indicator)
    scaling_factor = parameter_derivative / sharpness_divisor * usable_pair_indicator
    pair_coeff = scaling_factor * (exp_pos / denominator - 1.0)
    neg_weight = (scaling_factor[:, None] * exp_neg / denominator[:, None]).astype(jnp.bfloat16)
    grad_query = pair_coeff[:, None] * anchor_embedding_matrix + jnp.dot(
        neg_weight, contrast_sample_entries, preferred_element_type=jnp.float32
    )
    grad_neg = lax.dot_general(
        neg_weight, probe_entry_count, (((0,), (0,)), ((), ())), preferred_element_type=jnp.float32
    )
    return (loss_sum, grad_query, pair_coeff, grad_neg)


def back_top(grad_embed, unit, unit_scale, active, normed, w_out):
    inner_prod = jnp.sum(unit * grad_embed, axis=1, keepdims=True)
    grad_out = (unit_scale * (grad_embed - unit * inner_prod)).astype(jnp.bfloat16)
    grad_wo = lax.dot_general(
        active, grad_out, (((0,), (0,)), ((), ())), preferred_element_type=jnp.float32
    )
    grad_act = lax.dot_general(
        grad_out, w_out, (((1,), (1,)), ((), ())), preferred_element_type=jnp.float32
    )
    return (grad_wo, jnp.where(normed > 0, grad_act, 0.0))


def back_bottom(feat_rows, grad_norm, normed, inv_std, sum_grad, sum_cross, all_points, w_hidden):
    mean_grad = sum_grad / all_points
    mean_cross = sum_cross / all_points
    grad_linear = (inv_std * (grad_norm - mean_grad - normed * mean_cross)).astype(jnp.bfloat16)
    grad_wh = lax.dot_general(
        feat_rows, grad_linear, (((0,), (0,)), ((), ())), preferred_element_type=jnp.float32
    )
    grad_feat = lax.dot_general(
        grad_linear, w_hidden, (((1,), (1,)), ((), ())), preferred_element_type=jnp.float32
    )
    return (grad_feat.astype(jnp.bfloat16), grad_wh)


def body(feat_a, feat_b, w_hidden, w_out, send_rows, dest_rows, counts, neg_rows):
    points = feat_a.shape[2]
    feat_width = feat_a.shape[3]
    embed_width = w_out.shape[1]
    group_size = lax.axis_size("narrow")
    slot_count = send_rows.shape[3]
    all_points = lax.axis_size("wide") * group_size * points
    rows_a = feat_a.reshape(points, feat_width)
    rows_b = feat_b.reshape(points, feat_width)
    linear_a = jnp.dot(rows_a, w_hidden, preferred_element_type=jnp.float32)
    linear_b = jnp.dot(rows_b, w_hidden, preferred_element_type=jnp.float32)
    moments = (
        jnp.sum(linear_a, axis=0),
        jnp.sum(linear_a * linear_a, axis=0),
        jnp.sum(linear_b, axis=0),
        jnp.sum(linear_b * linear_b, axis=0),
    )
    pair_count = jnp.sum(counts).astype(jnp.float32)
    sum_a, square_a, sum_b, square_b = lax.psum(
        (moments[0], moments[1], moments[2], moments[3]), ("wide", "narrow")
    )
    normed_a, inv_std_a, active_a, scale_a, unit_a = finish(
        linear_a, sum_a, square_a, all_points, w_out
    )
    normed_b, inv_std_b, active_b, scale_b, unit_b = finish(
        linear_b, sum_b, square_b, all_points, w_out
    )
    embed_a = unit_a.astype(jnp.bfloat16)
    embed_b = unit_b.astype(jnp.bfloat16)
    sent_ids = send_rows.reshape(group_size * slot_count)
    keys_out = embed_b[sent_ids].reshape(group_size, slot_count, embed_width)
    got_keys, got_dest, got_count = (
        lax.all_to_all(keys_out, "narrow", split_axis=0, concat_axis=0, tiled=True),
        lax.all_to_all(
            dest_rows.reshape(group_size, slot_count),
            "narrow",
            split_axis=0,
            concat_axis=0,
            tiled=True,
        ),
        lax.all_to_all(
            counts.reshape(group_size), "narrow", split_axis=0, concat_axis=0, tiled=True
        ),
    )
    neg_ids = neg_rows.reshape(-1)
    contrast_sample_entries = lax.all_gather(embed_b[neg_ids], "narrow", axis=0, tiled=True)
    pair_total = lax.psum(pair_count, ("wide", "narrow"))
    parameter_derivative = jnp.float32(all_points) / pair_total
    pair_rows = group_size * slot_count
    usable_pair_indicator = (
        (jnp.arange(slot_count)[None, :] < got_count[:, None]).astype(jnp.float32).reshape(-1)
    )
    dest_flat = got_dest.reshape(-1)
    probe_entry_count = embed_a[dest_flat]
    key_rows = got_keys.reshape(pair_rows, embed_width)
    block_rows = min(1024, pair_rows)
    block_count = pair_rows // block_rows

    def one_block(running, part_rows):
        query_blk, key_blk, live_blk = part_rows
        loss_sum, grad_query, pair_coeff, grad_neg = pair_terms(
            query_blk, key_blk, live_blk, contrast_sample_entries, parameter_derivative
        )
        return ((running[0] + loss_sum, running[1] + grad_neg), (grad_query, pair_coeff))

    start_state = (
        jnp.zeros((), jnp.float32),
        jnp.zeros((contrast_sample_entries.shape[0], embed_width), jnp.float32),
    )
    blocks_in = (
        probe_entry_count.reshape(block_count, block_rows, embed_width),
        key_rows.reshape(block_count, block_rows, embed_width),
        usable_pair_indicator.reshape(block_count, block_rows),
    )
    (loss_local, grad_neg), (grad_query, pair_coeff) = lax.scan(one_block, start_state, blocks_in)
    grad_query = grad_query.reshape(pair_rows, embed_width)
    pair_coeff = pair_coeff.reshape(pair_rows)
    grad_embed_a = jax.ops.segment_sum(grad_query, dest_flat, num_segments=points)
    grad_sent = pair_coeff[:, None] * probe_entry_count.astype(jnp.float32)
    grad_key = (
        lax.all_to_all(
            grad_sent.reshape(group_size, slot_count, embed_width).astype(jnp.bfloat16),
            "narrow",
            split_axis=0,
            concat_axis=0,
            tiled=True,
        )
        .astype(jnp.float32)
        .reshape(pair_rows, embed_width)
    )
    grad_neg_mine = lax.psum_scatter(
        grad_neg.astype(jnp.bfloat16), "narrow", scatter_dimension=0, tiled=True
    ).astype(jnp.float32)
    grad_embed_b = jax.ops.segment_sum(
        grad_key, sent_ids, num_segments=points
    ) + jax.ops.segment_sum(grad_neg_mine, neg_ids, num_segments=points)
    wo_a, grad_norm_a = back_top(grad_embed_a, unit_a, scale_a, active_a, normed_a, w_out)
    wo_b, grad_norm_b = back_top(grad_embed_b, unit_b, scale_b, active_b, normed_b, w_out)
    grad_sum_a, cross_sum_a, grad_sum_b, cross_sum_b, loss_total = lax.psum(
        (
            jnp.sum(grad_norm_a, axis=0),
            jnp.sum(grad_norm_a * normed_a, axis=0),
            jnp.sum(grad_norm_b, axis=0),
            jnp.sum(grad_norm_b * normed_b, axis=0),
            loss_local,
        ),
        ("wide", "narrow"),
    )
    feat_grad_a, wh_a = back_bottom(
        rows_a, grad_norm_a, normed_a, inv_std_a, grad_sum_a, cross_sum_a, all_points, w_hidden
    )
    feat_grad_b, wh_b = back_bottom(
        rows_b, grad_norm_b, normed_b, inv_std_b, grad_sum_b, cross_sum_b, all_points, w_hidden
    )
    grad_wh, grad_wo = lax.psum((wh_a + wh_b, wo_a + wo_b), ("wide", "narrow"))
    loss = loss_total / pair_total
    return (
        loss,
        feat_grad_a.reshape(feat_a.shape),
        feat_grad_b.reshape(feat_b.shape),
        grad_wh,
        grad_wo,
    )


def solution(mesh):
    placed = (
        P("wide", "narrow", None, None),
        P("wide", "narrow", None, None),
        P(),
        P(),
        P("wide", "narrow", None, None),
        P("wide", "narrow", None, None),
        P("wide", "narrow", None),
        P("wide", "narrow", None),
    )
    return jax.shard_map(
        body,
        mesh=mesh,
        in_specs=placed,
        out_specs=(P(), P("wide", "narrow", None, None), P("wide", "narrow", None, None), P(), P()),
        check_vma=False,
    )
```

profile of v0, /device:TPU:1, one launch (start us, length us, event | category | flops | bytes accessed | tf_op | source)
XLA Modules:
  0.0 514.8 jit_solution(1434882934924849387)
XLA Ops:
  8.8 4.4 fusion.47
  17.7 68.9 %all-reduce.1 = (f32[512]{0:T(512)S(1)}, f32[512]{0:T(512)S(1)}, f32[512]{0:T(512)S(1)}, f32[512]{0:T(512)S(1)}, f32[]{:T(128)}) all-reduce(f32[512]{0:T(512)S(1)} %get-tuple-element.199, f32[512]{0:T(512)S(1)} %get-tuple-element.198, f32[512]{0:T(512)S(1)} %get-tuple-element.197, ...), channel_id=1, replica_groups=mesh['wide'=8,'narrow'=16] {'wide','narrow'}, use_global_device_ids=true, to_apply=%region_3.0 | all-reduce | flops 2049 | bytes 16392 | tf_op jit(solution)/shard_map/psum | solution.py:100
  96.0 4.1 all-to-all-start.2
  106.4 5.9 %all-to-all-start = ((s32[16,1,128]{2,1,0:T(1,128)}), s32[16,1,128]{2,1,0:T(1,128)S(1)}, u32[]{:S(2)}, u32[]{:S(2)}) async-start(s32[16,1,128]{2,1,0:T(1,128)} %bitcast.1), calls=%async_computation | async-start | bytes 16384 | tf_op jit(solution)/shard_map/all_to_all | solution.py:115
  112.3 9.0 %gather_fusion.1 = bf16[2048,256]{1,0:T(8,128)(2,1)} fusion(bf16[2048,256]{1,0:T(8,128)(2,1)S(1)} %copy.38, s32[2048]{0:T(1024)S(1)} %broadcast_clamp_fusion), kind=kCustom, calls=%fused_computation.1 | custom fusion | bytes 2105344 | tf_op jit(solution)/shard_map/gather | solution.py:112
  124.0 6.7 %all-to-all-start.1 = ((bf16[16,128,256]{2,1,0:T(8,128)(2,1)}), bf16[16,128,256]{2,1,0:T(8,128)(2,1)}, u32[]{:S(2)}, u32[]{:S(2)}) async-start(bf16[16,128,256]{2,1,0:T(8,128)(2,1)} %bitcast.120), calls=%async_computation.1 | async-start | bytes 2097152 | tf_op jit(solution)/shard_map/all_to_all | solution.py:114
  131.0 9.1 %gather_fusion = bf16[2048,256]{1,0:T(8,128)(2,1)} fusion(bf16[2048,256]{1,0:T(8,128)(2,1)S(1)} %copy.37, s32[2048]{0:T(1024)S(1)} %broadcast_clamp_fusion.1), kind=kCustom, calls=%fused_computation | custom fusion | bytes 2105344 | tf_op jit(solution)/shard_map/gather | solution.py:135
  140.1 5.4 %all-to-all-done.1 = bf16[16,128,256]{2,1,0:T(8,128)(2,1)} async-done(((bf16[16,128,256]{2,1,0:T(8,128)(2,1)}), bf16[16,128,256]{2,1,0:T(8,128)(2,1)}, u32[]{:S(2)}, u32[]{:S(2)}) %all-to-all-start.1) | async-done | bytes 1048608 | tf_op jit(solution)/shard_map/all_to_all | solution.py:114
  145.5 36.6 %while.19 = (s32[]{:T(128)}, f32[]{:T(128)}, f32[2048,256]{1,0:T(8,128)}, f32[2,1024,256]{2,1,0:T(8,128)}, f32[2,1024]{1,0:T(2,128)S(1)}, /*index=5*/bf16[2,1024...) while((s32[]{:T(128)}, f32[]{:T(128)}, ...), condition=%wide.region_16.17_spmd.clone, body=%wide.region_12.16_spmd.clone.sunk | while | flops 3236705280 | bytes 64570616 | solution.py:156
  157.9 4.9 convolution_add_fusion.4
  172.6 3.3 fusion.84
  175.9 5.5 %convolution_add_fusion.4 = f32[2048,256]{1,0:T(8,128)} fusion(bf16[1024,2048]{1,0:T(8,128)(2,1)} %copy-done.1, f32[2048,256]{1,0:T(8,128)} %get-tuple-element.347, pred[]{:T(512)S(6)} %compare.3, bf16[2,1024,256]{2,1,0:T(8,128)(2,1)S(1)} %copy-done.2, s32[]{:T(128)} %get-tuple-element.345), kind=kOutput, calls=%fused_computation.9.clone.1 | convolution fusion | flops 1074790400 | bytes 8912901 | tf_op jit(solution)/shard_map/while/body/eval_jaxpr/dot_general | solution.py:51
  184.8 13.4 %scatter_custom_fusion = f32[2048,256]{1,0:T(8,128)} fusion(s32[2048]{0:T(1024)S(1)} %bitcast.124, f32[2048,256]{1,0:T(8,128)} %bitcast.15, f32[]{:T(128)} %constant.69.clone.1), kind=kCustom, calls=%fused_computation.71 | custom fusion | flops 524288 | bytes 2097664 | tf_op jit(solution)/shard_map/scatter-add | solution.py:159
  202.5 4.5 all-to-all-start.3
  214.6 3.4 fusion.46
  218.0 4.4 all-to-all-done.3
  222.4 13.0 %scatter_custom_fusion.1 = f32[2048,256]{1,0:T(8,128)} fusion(s32[2048]{0:T(1024)S(1)} %bitcast.128, bf16[2048,256]{1,0:T(8,128)(2,1)S(1)} %bitcast.119, f32[]{:T(128)} %constant.69.clone.1), kind=kCustom, calls=%fused_computation.47 | custom fusion | flops 1048576 | bytes 3145732 | tf_op jit(solution)/shard_map/scatter-add | solution.py:175
  238.3 23.6 %reduce-scatter.2.cloned.1.call-done = bf16[128,256]{1,0:T(8,128)(2,1)} async-done(((bf16[2048,256]{1,0:T(8,128)(2,1)}), bf16[128,256]{1,0:T(8,128)(2,1)}) %reduce-scatter.2.cloned.1.call-update) | async-done | bytes 65552 | tf_op jit(solution)/shard_map/reduce_scatter | solution.py:172
  267.8 3.6 multiply_reduce_fusion.5
  273.6 3.4 fusion.45
  278.6 67.0 %all-reduce = (f32[]{:T(128)}, f32[512]{0:T(512)S(1)}, f32[512]{0:T(512)S(1)}, f32[512]{0:T(512)S(1)}, f32[512]{0:T(512)S(1)}) all-reduce(f32[]{:T(128)} %get-tuple-element.135, f32[512]{0:T(512)S(1)} %get-tuple-element.195, f32[512]{0:T(512)S(1)} %get-tuple-element.194, ...), channel_id=1, replica_groups=mesh['wide'=8,'narrow'=16] {'wide','narrow'}, use_global_device_ids=true, to_apply=%region_17.18 | all-reduce | flops 2049 | bytes 16392 | tf_op jit(solution)/shard_map/psum | solution.py:180
  345.6 4.8 multiply_convert_fusion
  359.4 4.3 fusion.13
  366.4 137.3 %all-reduce.5.cloned.1.call-done = (f32[512,512]{0,1:T(8,128)}, f32[512,256]{1,0:T(8,128)}) async-done(((f32[512,512]{0,1:T(8,128)}, f32[512,256]{1,0:T(8,128)}), (f32[512,512]{0,1:T(8,128)}, f32[512,256]{1,0:T(8,128)})) %all-reduce.5.cloned.1.call-update) | async-done | bytes 1572880 | tf_op jit(solution)/shard_map/psum | solution.py:196
  (133 shorter events, 85.7 us)
Async XLA Ops:
  7.2 6.0 %copy-start.23 = (bf16[512,512]{1,0:T(8,128)(2,1)S(1)}, bf16[512,512]{1,0:T(8,128)(2,1)}, u32[]{:S(2)}) copy-start(bf16[512,512]{1,0:T(8,128)(2,1)} %param.12) | copy-start | bytes 1572868
  7.2 138.3 %all-gather.3.cloned.1.call-start = ((), (), s32[]{:S(2)}) async-start(), calls=%async_computation.6 | async-start | bytes 1114112 | tf_op jit(solution)/shard_map/all_gather | solution.py:127
  8.8 4.4 copy-start.16
  13.2 3.3 copy-start.22
  13.2 73.5 %copy-start.19 = (bf16[512,256]{1,0:T(8,128)(2,1)S(1)}, bf16[512,256]{1,0:T(8,128)(2,1)}, u32[]{:S(2)}) copy-start(bf16[512,256]{1,0:T(8,128)(2,1)} %param.13) | copy-start | bytes 786436
  92.2 7.8 %copy-start.21 = (s32[1,1,16,128]{3,2,1,0:T(8,128)S(1)}, s32[1,1,16,128]{3,2,1,0:T(8,128)}, u32[]{:S(2)}) copy-start(s32[1,1,16,128]{3,2,1,0:T(8,128)} %param.14) | copy-start | bytes 24580
  96.0 10.4 %all-to-all-start.2 = ((s32[16,1,1]{2,1,0:T(1,128)}), s32[16,1,1]{2,1,0:T(1,128)S(1)}, u32[]{:S(2)}, u32[]{:S(2)}) async-start(s32[16,1,1]{2,1,0:T(1,128)} %copy.40), calls=%async_computation.2 | async-start | bytes 16384 | tf_op jit(solution)/shard_map/all_to_all | solution.py:122
  106.4 17.6 %all-to-all-start = ((s32[16,1,128]{2,1,0:T(1,128)}), s32[16,1,128]{2,1,0:T(1,128)S(1)}, u32[]{:S(2)}, u32[]{:S(2)}) async-start(s32[16,1,128]{2,1,0:T(1,128)} %bitcast.1), calls=%async_computation | async-start | bytes 16384 | tf_op jit(solution)/shard_map/all_to_all | solution.py:115
  124.0 21.5 %all-to-all-start.1 = ((bf16[16,128,256]{2,1,0:T(8,128)(2,1)}), bf16[16,128,256]{2,1,0:T(8,128)(2,1)}, u32[]{:S(2)}, u32[]{:S(2)}) async-start(bf16[16,128,256]{2,1,0:T(8,128)(2,1)} %bitcast.120), calls=%async_computation.1 | async-start | bytes 2097152 | tf_op jit(solution)/shard_map/all_to_all | solution.py:114
  130.7 131.2 %reduce-scatter.2.cloned.1.call-start = ((), (), s32[]{:S(2)}) async-start(), calls=%async_computation.5 | async-start | bytes 1114112 | tf_op jit(solution)/shard_map/reduce_scatter | solution.py:172
  145.5 3.1 copy-start.2
  150.5 4.1 copy-start.8
  163.5 3.1 copy-start.2
  168.5 4.1 copy-start.8
  198.2 3.0 copy-start.3
  202.5 19.9 %all-to-all-start.3 = ((bf16[16,128,256]{2,1,0:T(8,128)(2,1)}), bf16[16,128,256]{2,1,0:T(8,128)(2,1)S(1)}, u32[]{:S(2)}, u32[]{:S(2)}) async-start(bf16[16,128,256]{2,1,0:T(8,128)(2,1)} %fusion.16), calls=%async_computation.3 | async-start | bytes 2097152 | tf_op jit(solution)/shard_map/all_to_all | solution.py:162
  207.0 296.7 %all-reduce.5.cloned.1.call-start = ((), (), s32[]{:S(2)}) async-start(), calls=%async_computation.7 | async-start | bytes 3145728 | tf_op jit(solution)/shard_map/psum | solution.py:196
  207.3 3.5 copy-start.9
  267.8 3.6 copy-start.5
  273.6 3.4 copy-start.26
  345.6 6.1 %copy-start.15 = (f32[2048,512]{1,0:T(8,128)S(1)}, f32[2048,512]{1,0:T(8,128)}, u32[]{:S(2)}) copy-start(f32[2048,512]{1,0:T(8,128)} %get-tuple-element.252) | copy-start | bytes 12582916
  350.4 2.9 copy-start.11
  355.9 3.6 copy-start.24
  359.4 4.4 copy-start.14
  (13 other events, 26.0 us)
Sparse Core Ops, SparseCore 0:
  95.4 37.7 all-gather.2
  184.9 76.8 reduce-scatter.1
  358.2 145.4 all-reduce.4
where the time goes:
time: 516 us; the launch traced here: 515 us
  waiting for transfers between devices  172 us (33%)
  blocking collectives  136 us (26%)
  other arithmetic  58.1 us (11%)
  matrix products  57.2 us (11%)
  local copies, waits for them, and re-layouts  51.1 us (10%)
  starting transfers between devices  21.6 us (4%)
  between operations  17.9 us (3%)
    psum x1, waiting for transfers between devices, body(): grad_wh, grad_wo = lax.psum((wh_a + wh_b, wo_a + wo_b), ('wide', 'narrow'))  137 us
    psum x1, blocking collectives, body(): lax.psum((moments[0], moments[1], moments[2], moments[3]), ('wide', 'narr...  68.9 us
    psum x1, blocking collectives, body(): lax.psum((jnp.sum(grad_norm_a, axis=0), jnp.sum(grad_norm_a * normed_a, a...  67 us
    reduce_scatter x1, waiting for transfers between devices, body(): lax.psum_scatter(grad_neg.astype(jnp.bfloat16), 'narrow', scatter_dimensi...  23.6 us
    unnamed x51, local copies, waits for them, and re-layouts  14.9 us
    scatter-add x1, other arithmetic, body(): jax.ops.segment_sum(grad_query, dest_flat, num_segments=points)  13.4 us
    scatter-add x1, other arithmetic, body(): jax.ops.segment_sum(grad_key, sent_ids, num_segments=points)  13 us
    dot_general x2, matrix products, pair_terms(): lax.dot_general(neg_weight, probe_entry_count, (((0,), (0,)), ((), ())),...  10.4 us
  transfers between devices with their start and end apart: 7, of which 5 were waited for; matrix products, arithmetic and copies ran while one was open for 14% of the time, Pallas kernels for 0%

commit v1 on v0

--- a/solution.py
+++ b/solution.py
@@ -1,9 +1,209 @@
 import jax
 import jax.numpy as jnp
 from jax import lax
+from jax.experimental import pallas as pl
+from jax.experimental.pallas import tpu as pltpu
 from jax.sharding import PartitionSpec as P
 
 sharpness_divisor = 0.07
+MESH = pl.DeviceIdType.MESH
+GROUP = 16
+
+
+def small_sum_kernel(x_ref, o_ref, near, part, far, send_n, recv_n, send_w, recv_w):
+    w = lax.axis_index("wide")
+    n = lax.axis_index("narrow")
+    n_wide = far.shape[0]
+    n_narrow = near.shape[0]
+    barrier = pltpu.get_barrier_semaphore()
+    for d in range(1, n_narrow):
+        pl.semaphore_signal(
+            barrier, inc=1, device_id=(w, lax.rem(n + d, n_narrow)), device_id_type=MESH
+        )
+    for d in range(1, n_wide):
+        pl.semaphore_signal(
+            barrier, inc=1, device_id=(lax.rem(w + d, n_wide), n), device_id_type=MESH
+        )
+    pl.semaphore_wait(barrier, n_narrow + n_wide - 2)
+    first = [
+        pltpu.make_async_remote_copy(
+            src_ref=x_ref,
+            dst_ref=near.at[n],
+            send_sem=send_n.at[d],
+            recv_sem=recv_n.at[d],
+            device_id=(w, lax.rem(n + d, n_narrow)),
+            device_id_type=MESH,
+        )
+        for d in range(1, n_narrow)
+    ]
+    for copy in first:
+        copy.start()
+    near[n] = x_ref[...]
+    for copy in first:
+        copy.wait()
+    part[...] = jnp.sum(near[...], axis=0)
+    second = [
+        pltpu.make_async_remote_copy(
+            src_ref=part,
+            dst_ref=far.at[w],
+            send_sem=send_w.at[d],
+            recv_sem=recv_w.at[d],
+            device_id=(lax.rem(w + d, n_wide), n),
+            device_id_type=MESH,
+        )
+        for d in range(1, n_wide)
+    ]
+    for copy in second:
+        copy.start()
+    far[w] = part[...]
+    for copy in second:
+        copy.wait()
+    o_ref[...] = jnp.sum(far[...], axis=0)
+
+
+def small_sum(x, collective_id):
+    n_wide, n_narrow = lax.axis_size("wide"), lax.axis_size("narrow")
+    vmem = pl.BlockSpec(memory_space=pltpu.VMEM)
+    return pl.pallas_call(
+        small_sum_kernel,
+        out_shape=jax.ShapeDtypeStruct(x.shape, x.dtype),
+        in_specs=[vmem],
+        out_specs=vmem,
+        scratch_shapes=[
+            pltpu.VMEM((n_narrow,) + x.shape, x.dtype),
+            pltpu.VMEM(x.shape, x.dtype),
+            pltpu.VMEM((n_wide,) + x.shape, x.dtype),
+            pltpu.SemaphoreType.DMA((n_narrow,)),
+            pltpu.SemaphoreType.DMA((n_narrow,)),
+            pltpu.SemaphoreType.DMA((n_wide,)),
+            pltpu.SemaphoreType.DMA((n_wide,)),
+        ],
+        compiler_params=pltpu.CompilerParams(
+            collective_id=collective_id, has_side_effects=True
+        ),
+        name=f"small_sum_{collective_id}",
+    )(x)
+
+
+def grad_sum_kernel(
+    x_ref, o_ref, half, own, near, chunk, far, out, pair_sem, send_b, recv_b, send_c, recv_c, send_d, recv_d
+):
+    w = lax.axis_index("wide")
+    n = lax.axis_index("narrow")
+    n_narrow = near.shape[0]
+    n_z = far.shape[0]
+    rows = near.shape[1]
+    span = n_narrow * rows
+    z, c = w // 2, lax.rem(w, 2)
+    partner = (2 * z + 1 - c, n)
+    peers = [(w, lax.rem(n + d, n_narrow)) for d in range(1, n_narrow)]
+    stack = [(2 * lax.rem(z + d, n_z) + c, n) for d in range(1, n_z)]
+    barrier = pltpu.get_barrier_semaphore()
+    for device in [partner] + peers + stack:
+        pl.semaphore_signal(barrier, inc=1, device_id=device, device_id_type=MESH)
+    pl.semaphore_wait(barrier, n_narrow + n_z - 1)
+
+    def send(src, dst, send_sem, recv_sem, device):
+        return pltpu.make_async_remote_copy(
+            src_ref=src,
+            dst_ref=dst,
+            send_sem=send_sem,
+            recv_sem=recv_sem,
+            device_id=device,
+            device_id_type=MESH,
+        )
+
+    mine = pl.multiple_of(c * span, span)
+    other = pl.multiple_of((1 - c) * span, span)
+    swap = send(x_ref.at[pl.ds(other, span)], half, pair_sem.at[0], pair_sem.at[1], partner)
+    swap.start()
+    swap.wait()
+    own[...] = (
+        x_ref[pl.ds(mine, span), :].astype(jnp.float32) + half[...].astype(jnp.float32)
+    ).astype(jnp.bfloat16)
+    copies = [
+        send(
+            own.at[pl.ds(pl.multiple_of(peer[1] * rows, rows), rows)],
+            near.at[n],
+            send_b.at[d],
+            recv_b.at[d],
+            peer,
+        )
+        for d, peer in enumerate(peers)
+    ]
+    for copy in copies:
+        copy.start()
+    near[n] = own[pl.ds(pl.multiple_of(n * rows, rows), rows), :]
+    for copy in copies:
+        copy.wait()
+    chunk[...] = jnp.sum(near[...].astype(jnp.float32), axis=0).astype(jnp.bfloat16)
+    copies = [
+        send(chunk, far.at[z], send_c.at[d], recv_c.at[d], peer) for d, peer in enumerate(stack)
+    ]
+    for copy in copies:
+        copy.start()
+    far[z] = chunk[...]
+    for copy in copies:
+        copy.wait()
+    place = pl.multiple_of(mine + n * rows, rows)
+    out[pl.ds(place, rows), :] = jnp.sum(far[...].astype(jnp.float32), axis=0).astype(jnp.bfloat16)
+    copies = [
+        send(out.at[pl.ds(place, rows)], out.at[pl.ds(place, rows)], send_d.at[d], recv_d.at[d], peer)
+        for d, peer in enumerate(peers)
+    ]
+    for copy in copies:
+        copy.start()
+    for copy in copies:
+        copy.wait()
+    swap = send(
+        out.at[pl.ds(mine, span)], out.at[pl.ds(mine, span)], pair_sem.at[2], pair_sem.at[3], partner
+    )
+    swap.start()
+    swap.wait()
+    o_ref[...] = out[...].astype(jnp.float32)
+
+
+def grad_sum(wh, wo, collective_id):
+    n_narrow, n_z = lax.axis_size("narrow"), lax.axis_size("wide") // 2
+    width = wo.shape[1]
+    pieces = wh.shape[1] // width
+    x = jnp.concatenate(
+        [wh[:, i * width : (i + 1) * width] for i in range(pieces)] + [wo], axis=0
+    ).astype(jnp.bfloat16)
+    total = x.shape[0]
+    span = total // 2
+    rows = span // n_narrow
+    vmem = pl.BlockSpec(memory_space=pltpu.VMEM)
+    dma = pltpu.SemaphoreType.DMA
+    bf16 = jnp.bfloat16
+    got = pl.pallas_call(
+        grad_sum_kernel,
+        out_shape=jax.ShapeDtypeStruct(x.shape, jnp.float32),
+        in_specs=[vmem],
+        out_specs=vmem,
+        scratch_shapes=[
+            pltpu.VMEM((span, width), bf16),
+            pltpu.VMEM((span, width), bf16),
+            pltpu.VMEM((n_narrow, rows, width), bf16),
+            pltpu.VMEM((rows, width), bf16),
+            pltpu.VMEM((n_z, rows, width), bf16),
+            pltpu.VMEM((total, width), bf16),
+            dma((4,)),
+            dma((n_narrow,)),
+            dma((n_narrow,)),
+            dma((n_z,)),
+            dma((n_z,)),
+            dma((n_narrow,)),
+            dma((n_narrow,)),
+        ],
+        compiler_params=pltpu.CompilerParams(
+            collective_id=collective_id, has_side_effects=True, vmem_limit_bytes=32 * 1024 * 1024
+        ),
+        name="grad_sum",
+    )(x)
+    depth = wh.shape[0]
+    out_wh = jnp.concatenate([got[i * depth : (i + 1) * depth] for i in range(pieces)], axis=1)
+    return out_wh, got[pieces * depth :]
 
 
 def finish(linear, sum_lin, square_lin, all_points, w_out):
@@ -97,9 +297,11 @@
         jnp.sum(linear_b * linear_b, axis=0),
     )
     pair_count = jnp.sum(counts).astype(jnp.float32)
-    sum_a, square_a, sum_b, square_b = lax.psum(
-        (moments[0], moments[1], moments[2], moments[3]), ("wide", "narrow")
-    )
+    zero = jnp.zeros((3, moments[0].shape[0]), jnp.float32)
+    summed = small_sum(
+        jnp.concatenate([jnp.stack(moments), jnp.full_like(zero[:1], pair_count), zero]), 1
+    )
+    sum_a, square_a, sum_b, square_b = summed[0], summed[1], summed[2], summed[3]
     normed_a, inv_std_a, active_a, scale_a, unit_a = finish(
         linear_a, sum_a, square_a, all_points, w_out
     )
@@ -125,7 +327,7 @@
     )
     neg_ids = neg_rows.reshape(-1)
     contrast_sample_entries = lax.all_gather(embed_b[neg_ids], "narrow", axis=0, tiled=True)
-    pair_total = lax.psum(pair_count, ("wide", "narrow"))
+    pair_total = summed[4, 0]
     parameter_derivative = jnp.float32(all_points) / pair_total
     pair_rows = group_size * slot_count
     usable_pair_indicator = (
@@ -177,23 +379,23 @@
     ) + jax.ops.segment_sum(grad_neg_mine, neg_ids, num_segments=points)
     wo_a, grad_norm_a = back_top(grad_embed_a, unit_a, scale_a, active_a, normed_a, w_out)
     wo_b, grad_norm_b = back_top(grad_embed_b, unit_b, scale_b, active_b, normed_b, w_out)
-    grad_sum_a, cross_sum_a, grad_sum_b, cross_sum_b, loss_total = lax.psum(
-        (
-            jnp.sum(grad_norm_a, axis=0),
-            jnp.sum(grad_norm_a * normed_a, axis=0),
-            jnp.sum(grad_norm_b, axis=0),
-            jnp.sum(grad_norm_b * normed_b, axis=0),
-            loss_local,
-        ),
-        ("wide", "narrow"),
-    )
+    sums = [
+        jnp.sum(grad_norm_a, axis=0),
+        jnp.sum(grad_norm_a * normed_a, axis=0),
+        jnp.sum(grad_norm_b, axis=0),
+        jnp.sum(grad_norm_b * normed_b, axis=0),
+        jnp.full((zero.shape[1],), loss_local),
+    ]
+    back = small_sum(jnp.concatenate([jnp.stack(sums), zero]), 2)
+    grad_sum_a, cross_sum_a, grad_sum_b, cross_sum_b = back[0], back[1], back[2], back[3]
+    loss_total = back[4, 0]
     feat_grad_a, wh_a = back_bottom(
         rows_a, grad_norm_a, normed_a, inv_std_a, grad_sum_a, cross_sum_a, all_points, w_hidden
     )
     feat_grad_b, wh_b = back_bottom(
         rows_b, grad_norm_b, normed_b, inv_std_b, grad_sum_b, cross_sum_b, all_points, w_hidden
     )
-    grad_wh, grad_wo = lax.psum((wh_a + wh_b, wo_a + wo_b), ("wide", "narrow"))
+    grad_wh, grad_wo = grad_sum(wh_a + wh_b, wo_a + wo_b, 3)
     loss = loss_total / pair_total
     return (
         loss,

time: 516 us -> 304 us (0.59)
  waiting for transfers between devices: 172 us -> 32.5 us
  blocking collectives: 136 us -> 0 us
  Pallas kernels: 0 us -> 63.5 us
    psum x1 -> x0, waiting for transfers between devices: 137 us -> none  [body(): grad_wh, grad_wo = lax.psum((wh_a + wh_b, wo_a + wo_b), ('wide', 'narrow'))]
    psum x2 -> x0, blocking collectives: 136 us -> none  [the longest x1 68.9 us: body(): lax.psum((moments[0], moments[1], moments[2], moments[3]), ('wide', 'narr...]
    pallas_call x0 -> x3, Pallas kernels: none -> 63.5 us  [the longest x2 37.3 us: small_sum(): pl.pallas_call(small_sum_kernel, out_shape=jax.ShapeDtypeStruct(x.shape,...]
    unnamed x51 -> x43, local copies, waits for them, and re-layouts: 14.9 us -> 7.97 us
  transfers between devices with their start and end apart: 7 -> 6, of which waited for: 5 -> 3; matrix products, arithmetic and copies ran while one was open for 14% -> 23% of each run, Pallas kernels for 0% -> 0%
where the time goes in v1:
time: 304 us; the launch traced here: 303 us
  Pallas kernels  63.5 us (21%)
  other arithmetic  60.9 us (20%)
  matrix products  54.3 us (18%)
  local copies, waits for them, and re-layouts  50 us (16%)
  waiting for transfers between devices  32.5 us (11%)
  starting transfers between devices  22.2 us (7%)
  between operations  18.3 us (6%)
    pallas_call x2, Pallas kernels, small_sum(): pl.pallas_call(small_sum_kernel, out_shape=jax.ShapeDtypeStruct(x.shape,...  37.3 us
    pallas_call x1, Pallas kernels, grad_sum(): pl.pallas_call(grad_sum_kernel, out_shape=jax.ShapeDtypeStruct(x.shape, j...  26.2 us
    reduce_scatter x1, waiting for transfers between devices, body(): lax.psum_scatter(grad_neg.astype(jnp.bfloat16), 'narrow', scatter_dimensi...  26.1 us
    scatter-add x1, other arithmetic, body(): jax.ops.segment_sum(grad_query, dest_flat, num_segments=points)  13.4 us
    scatter-add x1, other arithmetic, body(): jax.ops.segment_sum(grad_key, sent_ids, num_segments=points)  13 us
    dot_general x2, matrix products, pair_terms(): lax.dot_general(neg_weight, probe_entry_count, (((0,), (0,)), ((), ())),...  10.4 us
    gather x1, local copies, waits for them, and re-layouts, body(): probe_entry_count = embed_a[dest_flat]  9.06 us
    gather x1, local copies, waits for them, and re-layouts, body(): keys_out = embed_b[sent_ids].reshape(group_size, slot_count, embed_width)  8.97 us
  transfers between devices with their start and end apart: 6, of which 3 were waited for; matrix products, arithmetic and copies ran while one was open for 23% of the time, Pallas kernels for 0%

profile of v1, /device:TPU:1, one launch (start us, length us, event | category | flops | bytes accessed | tf_op | source)
XLA Modules:
  0.0 303.1 jit_solution(14975349621395961835)
XLA Ops:
  7.2 5.1 %multiply_reduce_fusion.4 = (f32[512]{0:T(512)S(1)}, f32[512]{0:T(512)S(1)}, f32[2048,512]{1,0:T(8,128)}) fusion(bf16[512,512]{1,0:T(8,128)(2,1)} %param.12, bf16[1,1,2048,512]{3,2,1,0:T(8,128)(2,1)} %param.10), kind=kOutput, calls=%fused_computation.40 | convolution fusion | flops 1076886528 | bytes 6819840 | tf_op jit(solution)/shard_map/dot_general | solution.py:291
  12.3 3.2 %multiply_reduce_fusion.3 = (f32[512]{0:T(512)S(1)}, f32[512]{0:T(512)S(1)}, f32[2048,512]{1,0:T(8,128)}) fusion(bf16[512,512]{1,0:T(8,128)(2,1)S(1)} %copy-done.20, bf16[1,1,2048,512]{3,2,1,0:T(8,128)(2,1)S(1)} %copy-done), kind=kOutput, calls=%fused_computation.39 | convolution fusion | flops 1076886528 | bytes 6819840 | tf_op jit(solution)/shard_map/dot_general | solution.py:292
  17.5 19.6 %small_sum_1.1 = f32[8,512]{1,0:T(8,128)} custom-call(f32[8,512]{1,0:T(8,128)} %concatenate.13.x_ref), custom_call_target="tpu_custom_call" | custom-call | tf_op jit(solution)/shard_map/small_sum_1/pallas_call | solution.py:67
  47.2 5.1 %all-to-all-start.2 = ((s32[16,1,1]{2,1,0:T(1,128)}), s32[16,1,1]{2,1,0:T(1,128)S(1)}, u32[]{:S(2)}, u32[]{:S(2)}) async-start(s32[16,1,1]{2,1,0:T(1,128)} %copy.37), calls=%async_computation.2 | async-start | bytes 16384 | tf_op jit(solution)/shard_map/all_to_all | solution.py:324
  58.6 5.9 %all-to-all-start = ((s32[16,1,128]{2,1,0:T(1,128)}), s32[16,1,128]{2,1,0:T(1,128)S(1)}, u32[]{:S(2)}, u32[]{:S(2)}) async-start(s32[16,1,128]{2,1,0:T(1,128)} %bitcast.8), calls=%async_computation | async-start | bytes 16384 | tf_op jit(solution)/shard_map/all_to_all | solution.py:317
  68.1 9.0 %gather_fusion.1 = bf16[2048,256]{1,0:T(8,128)(2,1)} fusion(bf16[2048,256]{1,0:T(8,128)(2,1)S(1)} %copy.35, s32[2048]{0:T(1024)S(1)} %broadcast_clamp_fusion), kind=kCustom, calls=%fused_computation.1 | custom fusion | bytes 2105344 | tf_op jit(solution)/shard_map/gather | solution.py:314
  78.3 6.7 %all-to-all-start.1 = ((bf16[16,128,256]{2,1,0:T(8,128)(2,1)}), bf16[16,128,256]{2,1,0:T(8,128)(2,1)}, u32[]{:S(2)}, u32[]{:S(2)}) async-start(bf16[16,128,256]{2,1,0:T(8,128)(2,1)} %bitcast.140), calls=%async_computation.1 | async-start | bytes 2097152 | tf_op jit(solution)/shard_map/all_to_all | solution.py:316
  85.4 9.1 %gather_fusion = bf16[2048,256]{1,0:T(8,128)(2,1)} fusion(bf16[2048,256]{1,0:T(8,128)(2,1)S(1)} %copy-done.2, s32[2048]{0:T(1024)S(1)} %broadcast_clamp_fusion.1), kind=kCustom, calls=%fused_computation | custom fusion | bytes 2105344 | tf_op jit(solution)/shard_map/gather | solution.py:337
  94.4 5.6 %all-to-all-done.1 = bf16[16,128,256]{2,1,0:T(8,128)(2,1)} async-done(((bf16[16,128,256]{2,1,0:T(8,128)(2,1)}), bf16[16,128,256]{2,1,0:T(8,128)(2,1)}, u32[]{:S(2)}, u32[]{:S(2)}) %all-to-all-start.1) | async-done | bytes 1048608 | tf_op jit(solution)/shard_map/all_to_all | solution.py:316
  100.0 36.6 %while.19 = (s32[]{:T(128)}, f32[]{:T(128)}, f32[2048,256]{1,0:T(8,128)}, f32[2,1024,256]{2,1,0:T(8,128)}, f32[2,1024]{1,0:T(2,128)S(1)}, /*index=5*/bf16[2,1024...) while((s32[]{:T(128)}, f32[]{:T(128)}, ...), condition=%wide.region_11.12_spmd.clone, body=%wide.region_7.11_spmd.clone.sunk | while | flops 3236705280 | bytes 64570616 | solution.py:358
  109.1 3.3 %fusion.86 = f32[2,1024,256]{2,1,0:T(8,128)} fusion(f32[2,1024,256]{2,1,0:T(8,128)} %get-tuple-element.323, s32[]{:T(128)} %get-tuple-element.320, bf16[1024,2048]{1,0:T(8,128)(2,1)S(1)} %divide_convert_fusion.2, bf16[2048,256]{1,0:T(8,128)(2,1)S(1)} %copy-done.9, f32[1024]{0:T(1024)S(1)} %get-tuple-element.306, ...), kind=kOutput, calls=%fused_computation.14.clone.1 | convolution fusion | flops 1074528256 | bytes 6820352 | tf_op jit(solution)/shard_map/while/body/eval_jaxpr/dot_general | solution.py:248
  112.4 4.9 %convolution_add_fusion.4 = f32[2048,256]{1,0:T(8,128)} fusion(bf16[1024,2048]{1,0:T(8,128)(2,1)} %copy-done.1, f32[2048,256]{1,0:T(8,128)} %get-tuple-element.322, pred[]{:T(512)S(6)} %compare.3, bf16[2,1024,256]{2,1,0:T(8,128)(2,1)S(1)} %copy-done.3, s32[]{:T(128)} %get-tuple-element.320), kind=kOutput, calls=%fused_computation.9.clone.1 | convolution fusion | flops 1074790400 | bytes 8912901 | tf_op jit(solution)/shard_map/while/body/eval_jaxpr/dot_general | solution.py:251
  127.1 3.3 %fusion.86 = f32[2,1024,256]{2,1,0:T(8,128)} fusion(f32[2,1024,256]{2,1,0:T(8,128)} %get-tuple-element.323, s32[]{:T(128)} %get-tuple-element.320, bf16[1024,2048]{1,0:T(8,128)(2,1)S(1)} %divide_convert_fusion.2, bf16[2048,256]{1,0:T(8,128)(2,1)S(1)} %copy-done.9, f32[1024]{0:T(1024)S(1)} %get-tuple-element.306, ...), kind=kOutput, calls=%fused_computation.14.clone.1 | convolution fusion | flops 1074528256 | bytes 6820352 | tf_op jit(solution)/shard_map/while/body/eval_jaxpr/dot_general | solution.py:248
  130.4 5.5 %convolution_add_fusion.4 = f32[2048,256]{1,0:T(8,128)} fusion(bf16[1024,2048]{1,0:T(8,128)(2,1)} %copy-done.1, f32[2048,256]{1,0:T(8,128)} %get-tuple-element.322, pred[]{:T(512)S(6)} %compare.3, bf16[2,1024,256]{2,1,0:T(8,128)(2,1)S(1)} %copy-done.3, s32[]{:T(128)} %get-tuple-element.320), kind=kOutput, calls=%fused_computation.9.clone.1 | convolution fusion | flops 1074790400 | bytes 8912901 | tf_op jit(solution)/shard_map/while/body/eval_jaxpr/dot_general | solution.py:251
  140.8 4.2 %all-to-all-start.3 = ((bf16[16,128,256]{2,1,0:T(8,128)(2,1)}), bf16[16,128,256]{2,1,0:T(8,128)(2,1)S(1)}, u32[]{:S(2)}, u32[]{:S(2)}) async-start(bf16[16,128,256]{2,1,0:T(8,128)(2,1)} %fusion.16), calls=%async_computation.3 | async-start | bytes 2097152 | tf_op jit(solution)/shard_map/all_to_all | solution.py:364
  145.0 13.4 %scatter_custom_fusion = f32[2048,256]{1,0:T(8,128)} fusion(s32[2048]{0:T(1024)S(1)} %bitcast.144, f32[2048,256]{1,0:T(8,128)} %bitcast.24, f32[]{:T(128)} %constant.71.clone.1), kind=kCustom, calls=%fused_computation.74 | custom fusion | flops 524288 | bytes 2097664 | tf_op jit(solution)/shard_map/scatter-add | solution.py:361
  168.6 3.4 %multiply_reduce_fusion.2 = (f32[512]{0:T(512)S(1)}, f32[512]{0:T(512)S(1)}, f32[2048,512]{1,0:T(8,128)}) fusion(f32[2048,512]{1,0:T(8,128)S(1)} %copy-done.13, f32[512]{0:T(512)S(1)} %bitcast.157, f32[512]{0:T(512)S(1)} %bitcast.161, bf16[2048,256]{0,1:T(8,128)(2,1)S(1)} %multiply_convert_fusion.3, bf16[512,256]{1,0:T(8,128)(2,1)S(1)} %copy-done.16), kind=kOutput, calls=%fused_computation.34 | convolution fusion | flops 544209920 | bytes 9707520 | tf_op jit(solution)/shard_map/dot_general | solution.py:263
  172.0 13.0 %scatter_custom_fusion.1 = f32[2048,256]{1,0:T(8,128)} fusion(s32[2048]{0:T(1024)S(1)} %bitcast.168, bf16[2048,256]{1,0:T(8,128)(2,1)S(1)} %bitcast.139, f32[]{:T(128)} %constant.71.clone.1), kind=kCustom, calls=%fused_computation.47 | custom fusion | flops 1048576 | bytes 3145732 | tf_op jit(solution)/shard_map/scatter-add | solution.py:377
  187.9 26.1 %reduce-scatter.2.cloned.1.call-done = bf16[128,256]{1,0:T(8,128)(2,1)} async-done(((bf16[2048,256]{1,0:T(8,128)(2,1)}), bf16[128,256]{1,0:T(8,128)(2,1)}) %reduce-scatter.2.cloned.1.call-update) | async-done | bytes 65552 | tf_op jit(solution)/shard_map/reduce_scatter | solution.py:374
  219.9 3.6 %multiply_reduce_fusion.5 = (f32[2048]{0:T(1024)S(1)}, f32[2048,256]{0,1:T(8,128)S(1)}) fusion(f32[2048,256]{0,1:T(8,128)} %copy-done.5, f32[2048]{0:T(1024)S(1)} %add_rsqrt_fusion, f32[2048,256]{0,1:T(8,128)} %copy.40, f32[2048,256]{0,1:T(8,128)} %copy.41), kind=kLoop, calls=%fused_computation.60 | loop fusion | flops 2095104 | bytes 8404992 | tf_op jit(solution)/shard_map/reduce_sum | solution.py:258
  225.7 3.3 %multiply_reduce_fusion.1 = (f32[512]{0:T(512)S(1)}, f32[512]{0:T(512)S(1)}, f32[2048,512]{1,0:T(8,128)}) fusion(f32[2048,512]{1,0:T(8,128)S(1)} %copy-done.11, f32[512]{0:T(512)S(1)} %bitcast.152, f32[512]{0:T(512)S(1)} %bitcast.148, bf16[2048,256]{0,1:T(8,128)(2,1)S(1)} %multiply_convert_fusion.2, bf16[512,256]{1,0:T(8,128)(2,1)S(1)} %copy-done.16), kind=kOutput, calls=%fused_computation.33 | convolution fusion | flops 544209920 | bytes 9707520 | tf_op jit(solution)/shard_map/dot_general | solution.py:263
  229.6 17.7 %small_sum_2.1 = f32[8,512]{1,0:T(8,128)} custom-call(f32[8,512]{1,0:T(8,128)} %concatenate.14.x_ref), custom_call_target="tpu_custom_call" | custom-call | tf_op jit(solution)/shard_map/small_sum_2/pallas_call | solution.py:67
  248.2 4.6 %multiply_convert_fusion = bf16[2048,512]{1,0:T(8,128)(2,1)S(1)} fusion(f32[2048,512]{1,0:T(8,128)} %get-tuple-element.230, f32[2048,512]{1,0:T(8,128)} %get-tuple-element.224, f32[512]{0:T(512)S(1)} %bitcast.166, f32[512]{0:T(512)S(1)} %bitcast.165, f32[512]{0:T(512)S(1)} %bitcast.153, f32[512]{0:T(512)S(1)} %bitcast.149), kind=kLoop, calls=%fused_computation.31 | loop fusion | flops 7340032 | bytes 10493952 | tf_op jit(solution)/shard_map/convert_element_type | solution.py:272
  265.6 26.2 %grad_sum.1 = f32[1536,256]{1,0:T(8,128)S(1)} custom-call(bf16[1536,256]{1,0:T(8,128)(2,1)S(1)} %pad_maximum_fusion.1.x_ref), custom_call_target="tpu_custom_call" | custom-call | tf_op jit(solution)/shard_map/grad_sum/pallas_call | solution.py:179
  (131 shorter events, 81.7 us)
Async XLA Ops:
  7.2 5.1 %copy-start = (bf16[1,1,2048,512]{3,2,1,0:T(8,128)(2,1)S(1)}, bf16[1,1,2048,512]{3,2,1,0:T(8,128)(2,1)}, u32[]{:S(2)}) copy-start(bf16[1,1,2048,512]{3,2,1,0:T(8,128)(2,1)} %param.11) | copy-start | bytes 6291460
  7.2 5.1 %copy-start.20 = (bf16[512,512]{1,0:T(8,128)(2,1)S(1)}, bf16[512,512]{1,0:T(8,128)(2,1)}, u32[]{:S(2)}) copy-start(bf16[512,512]{1,0:T(8,128)(2,1)} %param.12) | copy-start | bytes 1572868
  7.2 92.8 %all-gather.3.cloned.1.call-start = ((), (), s32[]{:S(2)}) async-start(), calls=%async_computation.6 | async-start | bytes 1114112 | tf_op jit(solution)/shard_map/all_gather | solution.py:329
  12.3 3.2 %copy-start.18 = (s32[1,1,16]{2,1,0:T(1,128)S(1)}, s32[1,1,16]{2,1,0:T(1,128)}, u32[]{:S(2)}) copy-start(s32[1,1,16]{2,1,0:T(1,128)} %param.16) | copy-start | bytes 196
  12.3 25.6 %copy-start.16 = (bf16[512,256]{1,0:T(8,128)(2,1)S(1)}, bf16[512,256]{1,0:T(8,128)(2,1)}, u32[]{:S(2)}) copy-start(bf16[512,256]{1,0:T(8,128)(2,1)} %param.13) | copy-start | bytes 786436
  42.3 2.6 copy-start.22
  47.2 11.5 %all-to-all-start.2 = ((s32[16,1,1]{2,1,0:T(1,128)}), s32[16,1,1]{2,1,0:T(1,128)S(1)}, u32[]{:S(2)}, u32[]{:S(2)}) async-start(s32[16,1,1]{2,1,0:T(1,128)} %copy.37), calls=%async_computation.2 | async-start | bytes 16384 | tf_op jit(solution)/shard_map/all_to_all | solution.py:324
  52.3 3.1 %copy-start.17 = (s32[1,1,16,128]{3,2,1,0:T(8,128)S(1)}, s32[1,1,16,128]{3,2,1,0:T(8,128)}, u32[]{:S(2)}) copy-start(s32[1,1,16,128]{3,2,1,0:T(8,128)} %param.14) | copy-start | bytes 24580
  58.6 19.6 %all-to-all-start = ((s32[16,1,128]{2,1,0:T(1,128)}), s32[16,1,128]{2,1,0:T(1,128)S(1)}, u32[]{:S(2)}, u32[]{:S(2)}) async-start(s32[16,1,128]{2,1,0:T(1,128)} %bitcast.8), calls=%async_computation | async-start | bytes 16384 | tf_op jit(solution)/shard_map/all_to_all | solution.py:317
  77.1 8.3 %copy-start.2 = (bf16[2048,256]{1,0:T(8,128)(2,1)S(1)}, bf16[2048,256]{1,0:T(8,128)(2,1)}, u32[]{:S(2)}) copy-start(bf16[2048,256]{1,0:T(8,128)(2,1)} %copy.34) | copy-start | bytes 3145732
  78.3 21.7 %all-to-all-start.1 = ((bf16[16,128,256]{2,1,0:T(8,128)(2,1)}), bf16[16,128,256]{2,1,0:T(8,128)(2,1)}, u32[]{:S(2)}, u32[]{:S(2)}) async-start(bf16[16,128,256]{2,1,0:T(8,128)(2,1)} %bitcast.140), calls=%async_computation.1 | async-start | bytes 2097152 | tf_op jit(solution)/shard_map/all_to_all | solution.py:316
  85.0 129.0 %reduce-scatter.2.cloned.1.call-start = ((), (), s32[]{:S(2)}) async-start(), calls=%async_computation.5 | async-start | bytes 1114112 | tf_op jit(solution)/shard_map/reduce_scatter | solution.py:374
  100.0 3.1 %copy-start.3 = (bf16[2,1024,256]{2,1,0:T(8,128)(2,1)S(1)}, bf16[2,1024,256]{2,1,0:T(8,128)(2,1)}, u32[]{:S(2)}) copy-start(bf16[2,1024,256]{2,1,0:T(8,128)(2,1)} %get-tuple-element.337) | copy-start | bytes 3145732 | tf_op jit(solution)/shard_map/while
  105.0 4.1 %copy-start.9 = (bf16[2048,256]{1,0:T(8,128)(2,1)S(1)}, bf16[2048,256]{1,0:T(8,128)(2,1)}, u32[]{:S(2)}) copy-start(bf16[2048,256]{1,0:T(8,128)(2,1)} %get-tuple-element.339) | copy-start | bytes 3145732 | tf_op jit(solution)/shard_map/while
  118.0 3.1 %copy-start.3 = (bf16[2,1024,256]{2,1,0:T(8,128)(2,1)S(1)}, bf16[2,1024,256]{2,1,0:T(8,128)(2,1)}, u32[]{:S(2)}) copy-start(bf16[2,1024,256]{2,1,0:T(8,128)(2,1)} %get-tuple-element.337) | copy-start | bytes 3145732 | tf_op jit(solution)/shard_map/while
  123.0 4.1 %copy-start.9 = (bf16[2048,256]{1,0:T(8,128)(2,1)S(1)}, bf16[2048,256]{1,0:T(8,128)(2,1)}, u32[]{:S(2)}) copy-start(bf16[2048,256]{1,0:T(8,128)(2,1)} %get-tuple-element.339) | copy-start | bytes 3145732 | tf_op jit(solution)/shard_map/while
  136.6 2.8 copy-start.4
  140.8 31.2 %all-to-all-start.3 = ((bf16[16,128,256]{2,1,0:T(8,128)(2,1)}), bf16[16,128,256]{2,1,0:T(8,128)(2,1)S(1)}, u32[]{:S(2)}, u32[]{:S(2)}) async-start(bf16[16,128,256]{2,1,0:T(8,128)(2,1)} %fusion.16), calls=%async_computation.3 | async-start | bytes 2097152 | tf_op jit(solution)/shard_map/all_to_all | solution.py:364
  161.3 2.9 copy-start.8
  161.3 3.5 %copy-start.10 = (f32[2048,256]{0,1:T(8,128)S(1)}, f32[2048,256]{0,1:T(8,128)}, u32[]{:S(2)}) copy-start(f32[2048,256]{0,1:T(8,128)} %copy.39) | copy-start | bytes 6291460
  219.9 3.6 %copy-start.6 = (f32[2048,256]{0,1:T(8,128)S(1)}, f32[2048,256]{0,1:T(8,128)}, u32[]{:S(2)}) copy-start(f32[2048,256]{0,1:T(8,128)} %copy-done.5) | copy-start | bytes 6291460
  254.2 4.4 %copy-start.14 = (f32[2048,512]{1,0:T(8,128)S(1)}, f32[2048,512]{1,0:T(8,128)}, u32[]{:S(2)}) copy-start(f32[2048,512]{1,0:T(8,128)} %get-tuple-element.223) | copy-start | bytes 12582916
  254.2 4.4 %copy-start.15 = (f32[2048,512]{1,0:T(8,128)S(1)}, f32[2048,512]{1,0:T(8,128)}, u32[]{:S(2)}) copy-start(f32[2048,512]{1,0:T(8,128)} %get-tuple-element.229) | copy-start | bytes 12582916
  259.8 2.6 copy-start.19
  (9 other events, 16.8 us)
Sparse Core Ops, SparseCore 0:
  46.6 39.1 all-gather.2
  139.6 74.3 reduce-scatter.1

commit v2 on v0

v2 whole, which is shorter than its diff:
```python
import functools
import math

import jax
import jax.numpy as jnp
from jax import lax
from jax.experimental import pallas as pl
from jax.experimental.pallas import tpu as pltpu
from jax.sharding import PartitionSpec as P

MESH = pl.DeviceIdType.MESH
F32 = jnp.float32
BF16 = jnp.bfloat16
TEMPERATURE = 0.07
NT = (((1,), (1,)), ((), ()))
TN = (((0,), (0,)), ((), ()))


def dot(left, right, dims=None):
    if dims is None:
        return jnp.dot(left, right, preferred_element_type=F32)
    return lax.dot_general(left, right, dims, preferred_element_type=F32)


def one_hot(mask):
    return jnp.where(mask, 1.0, 0.0).astype(F32)


def fold(values):
    rows, width = values.shape
    return jnp.sum(values.reshape(rows // 8, 8, width), axis=0)


def remote(src, dst, sems, d, device):
    return pltpu.make_async_remote_copy(
        src_ref=src,
        dst_ref=dst,
        send_sem=sems.at[0, d],
        recv_sem=sems.at[1, d],
        device_id=device,
        device_id_type=MESH,
    )


def start_all(make, count):
    @pl.loop(1, count)
    def _(d):
        make(d).start()


def wait_all(make, count):
    @pl.loop(1, count)
    def _(d):
        make(d).wait()


def step_kernel(
    all_points,
    feat_a,
    feat_b,
    w_hidden,
    w_out,
    send_col,
    send_row,
    msg,
    neg_col,
    neg_row,
    loss_o,
    grad_feat_a,
    grad_feat_b,
    grad_wh_o,
    grad_wo_o,
    lin,
    normed,
    embed,
    scale,
    acc,
    stat,
    near,
    part,
    far,
    total,
    near2,
    part2,
    far2,
    total2,
    msg_in,
    dest_row,
    dest_col,
    negs,
    keys_out,
    keys_in,
    expo,
    exp_sum,
    num,
    spread,
    grad_rows,
    grad_out_slots,
    grad_in_slots,
    neg_out,
    neg_in,
    neg_mine,
    grad_norm,
    wo_acc,
    wh_acc,
    loss_acc,
    grads,
    half,
    own,
    piece,
    chunk,
    stack_in,
    merged,
    sem_msg,
    sem_near,
    sem_far,
    sem_near2,
    sem_far2,
    sem_neg,
    sem_key,
    sem_grad,
    sem_negback,
    sem_pair,
    sem_piece,
    sem_stack,
    sem_gather,
):
    w = lax.axis_index("wide")
    n = lax.axis_index("narrow")
    n_wide = far.shape[0]
    n_narrow = near.shape[0]
    n_z = stack_in.shape[0]
    points, _ = feat_a.shape
    hidden = w_hidden.shape[1]
    width = w_out.shape[1]
    cap = points // n_narrow
    neg_count = neg_col.shape[0]
    block = min(512, points)
    small = min(256, points)
    feats = (feat_a, feat_b)
    out_feats = (grad_feat_a, grad_feat_b)

    def peer(d):
        return (w, lax.rem(n + d, n_narrow))

    def across(d):
        return (lax.rem(w + d, n_wide), n)

    def rows_of(i, size):
        return pl.ds(pl.multiple_of(i * size, size), size)

    barrier = pltpu.get_barrier_semaphore()

    @pl.loop(1, n_narrow)
    def _(d):
        pl.semaphore_signal(barrier, inc=1, device_id=peer(d), device_id_type=MESH)

    @pl.loop(1, n_wide)
    def _(d):
        pl.semaphore_signal(barrier, inc=1, device_id=across(d), device_id_type=MESH)

    acc[...] = jnp.zeros_like(acc)
    for v in range(2):

        @pl.loop(0, points // block)
        def _(i):
            rows = rows_of(i, block)
            linear = dot(feats[v][rows, :], w_hidden[...])
            lin[v, rows, :] = linear
            acc[2 * v] += fold(linear)
            acc[2 * v + 1] += fold(linear * linear)

    stat[...] = jnp.zeros_like(stat)
    stat[0:4, :] = jnp.sum(acc[...], axis=1)
    stat[4:5, 0:cap] = jnp.sum(msg[:, 1, :].astype(F32), axis=0, keepdims=True)

    pl.semaphore_wait(barrier, n_narrow + n_wide - 2)

    def sum_all(near, part, far, total, sem_near, sem_far, between=None):
        def to_near(d):
            return remote(stat, near.at[n], sem_near, d, peer(d))

        def to_far(d):
            return remote(part, far.at[w], sem_far, d, across(d))

        start_all(to_near, n_narrow)
        near[n] = stat[...]
        if between is not None:
            between()
        wait_all(to_near, n_narrow)
        part[...] = jnp.sum(near[...], axis=0)
        start_all(to_far, n_wide)
        far[w] = part[...]
        wait_all(to_far, n_wide)
        total[...] = jnp.sum(far[...], axis=0)

    def to_msg(d):
        return remote(msg.at[lax.rem(n + d, n_narrow)], msg_in.at[n], sem_msg, d, peer(d))

    def send_msg():
        start_all(to_msg, n_narrow)
        msg_in[n] = msg[n]

    sum_all(near, part, far, total, sem_near, sem_far, send_msg)

    inv_count = 1.0 / all_points
    means, inverses = [], []
    for v in range(2):
        mean = total[2 * v : 2 * v + 1, :] * inv_count
        square = total[2 * v + 1 : 2 * v + 2, :] * inv_count
        means.append(mean)
        inverses.append(lax.rsqrt(square - mean * mean + 1e-5))

    def finish(v):
        @pl.loop(0, points // block)
        def _(i):
            rows = rows_of(i, block)
            value = ((lin[v, rows, :] - means[v]) * inverses[v]).astype(BF16)
            normed[v, rows, :] = value
            out = dot(jnp.maximum(value, 0), w_out[...])
            unit_scale = lax.rsqrt(jnp.sum(out * out, axis=1, keepdims=True) + 1e-6)
            embed[v, rows, :] = (out * unit_scale).astype(BF16)
            scale[v, rows, :] = unit_scale

    finish(1)
    lanes = lax.broadcasted_iota(jnp.int32, (neg_count, points), 1)
    my_negs = rows_of(n, neg_count)
    negs[my_negs, :] = dot(one_hot(neg_col[...] == lanes).astype(BF16), embed[1]).astype(BF16)

    def to_negs(d):
        return remote(negs.at[my_negs], negs.at[my_negs], sem_neg, d, peer(d))

    start_all(to_negs, n_narrow)

    batch = block // cap

    def to_key(d):
        return remote(
            keys_out.at[rows_of(lax.rem(n + d, n_narrow), cap)],
            keys_in.at[rows_of(n, cap)],
            sem_key,
            d,
            peer(d),
        )

    def gather(ids, table, i):
        lanes = lax.broadcasted_iota(jnp.int32, (cap, points), 1)
        picks = [
            one_hot(ids[rows_of(lax.rem(n + i * batch + k, n_narrow), cap), :] == lanes).astype(BF16)
            for k in range(batch)
        ]
        return dot(jnp.concatenate(picks, axis=0), table).astype(BF16)

    def permute_and_send(ids, table, out_ref, in_ref, make):
        @pl.loop(0, n_narrow // batch)
        def _(i):
            picked = gather(ids, table[...], i)
            for k in range(batch):
                d = i * batch + k
                out_ref[rows_of(lax.rem(n + d, n_narrow), cap), :] = picked[k * cap : (k + 1) * cap]

                @pl.when(d > 0)
                def _():
                    make(d).start()

        in_ref[rows_of(n, cap), :] = out_ref[rows_of(n, cap), :]

    permute_and_send(send_col, embed.at[1], keys_out, keys_in, to_key)

    finish(0)

    wait_all(to_msg, n_narrow)
    ids = msg_in[:, 0, :]
    slot = lax.broadcasted_iota(jnp.int32, ids.shape, 1)
    ids = jnp.where(slot < msg_in[:, 1, :], ids, ids + 2 * points)
    dest_row[...] = ids
    square_ids = jnp.concatenate(
        [ids.astype(F32), jnp.zeros((cap - n_narrow, cap), F32)], axis=0
    ).T.astype(jnp.int32)
    for s in range(n_narrow):
        dest_col[s * cap : (s + 1) * cap, :] = square_ids[:, s : s + 1]

    wait_all(to_negs, n_narrow)

    to_exp2 = math.log2(math.e) / TEMPERATURE

    @pl.loop(0, points // small)
    def _(i):
        rows = rows_of(i, small)
        score = dot(embed[0, rows, :], negs[...], NT)
        power = jnp.exp2(score * to_exp2)
        exp_sum[rows, :] = jnp.sum(power, axis=1, keepdims=True)
        power = power.astype(BF16)
        expo[rows, :] = power
        num[rows, :] = dot(power, negs[...])

    wait_all(to_key, n_narrow)

    pair_total = total[4:5, 0:1]
    weight = all_points / (pair_total * TEMPERATURE)
    loss_acc[...] = jnp.zeros_like(loss_acc)

    def rows_one_hot(row_ids, i, size, with_sum=False):
        place = lax.broadcasted_iota(jnp.int32, (size, cap), 0) + i * size
        picks = []
        hits = None
        for s in range(row_ids.shape[0]):
            hit = one_hot(row_ids[s : s + 1, :] == place)
            if with_sum:
                hits = hit if hits is None else hits + hit
            picks.append(hit.astype(BF16))
        picks = jnp.concatenate(picks, axis=1)
        return (picks, hits) if with_sum else picks

    @pl.loop(0, points // small)
    def _(i):
        rows = rows_of(i, small)
        picks, hits = rows_one_hot(dest_row, i, small, True)
        live = jnp.sum(hits, axis=1, keepdims=True)
        key = dot(picks, keys_in[...])
        query = embed[0, rows, :].astype(F32)
        positive = jnp.sum(query * key, axis=1, keepdims=True) * (1.0 / TEMPERATURE)
        exp_pos = jnp.exp(positive)
        denominator = exp_pos + exp_sum[rows, :]
        term = live * (jnp.log(denominator) - positive)
        loss_acc[...] += jnp.sum(term, axis=0, keepdims=True)
        share = live * weight / denominator
        pair_coeff = share * exp_pos - live * weight
        num[rows, :] = pair_coeff * key + share * num[rows, :]
        grad_rows[rows, :] = (pair_coeff * query).astype(BF16)
        spread[:, rows] = (share * query).T.astype(BF16)

    def to_slot(d):
        return remote(
            grad_out_slots.at[rows_of(lax.rem(n + d, n_narrow), cap)],
            grad_in_slots.at[rows_of(n, cap)],
            sem_grad,
            d,
            peer(d),
        )

    permute_and_send(dest_col, grad_rows, grad_out_slots, grad_in_slots, to_slot)

    def to_owner(d):
        return remote(
            neg_out.at[lax.rem(n + d, n_narrow)], neg_in.at[n], sem_negback, d, peer(d)
        )

    @pl.loop(0, n_narrow // batch)
    def _(i):
        for k in range(batch):
            d = i * batch + k
            owner = lax.rem(n + d, n_narrow)
            neg_out[owner] = dot(spread[...], expo[:, rows_of(owner, neg_count)]).T.astype(BF16)

            @pl.when(d > 0)
            def _():
                to_owner(d).start()

    neg_in[n] = neg_out[n]

    acc[...] = jnp.zeros_like(acc)
    wo_acc[...] = jnp.zeros_like(wo_acc)

    def back_top(v, grad_embed):
        @pl.loop(0, points // block)
        def _(i):
            rows = rows_of(i, block)
            grad = grad_embed(i, rows)
            unit = embed[v, rows, :].astype(F32)
            inner = jnp.sum(unit * grad, axis=1, keepdims=True)
            grad_out = (scale[v, rows, :] * (grad - unit * inner)).astype(BF16)
            value = normed[v, rows, :]
            wo_acc[...] += dot(grad_out, jnp.maximum(value, 0), TN)
            value = value.astype(F32)
            grad_act = jnp.where(value > 0, dot(grad_out, w_out[...], NT), 0.0)
            grad_norm[v, rows, :] = grad_act.astype(BF16)
            acc[2 * v] += fold(grad_act)
            acc[2 * v + 1] += fold(grad_act * value)

    back_top(0, lambda i, rows: num[rows, :])

    wait_all(to_slot, n_narrow)
    wait_all(to_owner, n_narrow)
    neg_mine[...] = jnp.sum(neg_in[...].astype(F32), axis=0).astype(BF16)

    def grad_b(i, rows):
        return dot(rows_one_hot(send_row, i, block), grad_in_slots[...]) + dot(
            rows_one_hot(neg_row, i, block), neg_mine[...]
        )

    back_top(1, grad_b)

    stat[0:4, :] = jnp.sum(acc[...], axis=1)
    stat[4:5, 0:cap] = loss_acc[0:1, :]
    sum_all(near2, part2, far2, total2, sem_near2, sem_far2)

    loss_o[...] = jnp.broadcast_to(total2[4:5, 0:cap] / pair_total, loss_o.shape)
    wh_acc[...] = jnp.zeros_like(wh_acc)
    for v in range(2):
        mean_grad = total2[2 * v : 2 * v + 1, :] * inv_count
        mean_cross = total2[2 * v + 1 : 2 * v + 2, :] * inv_count

        @pl.loop(0, points // block)
        def _(i):
            rows = rows_of(i, block)
            grad = grad_norm[v, rows, :].astype(F32)
            value = normed[v, rows, :].astype(F32)
            grad = (inverses[v] * (grad - mean_grad - value * mean_cross)).astype(BF16)
            grad_norm[v, rows, :] = grad
            wh_acc[...] += dot(feats[v][rows, :], grad, TN)

    depth = wh_acc.shape[0]
    parts = hidden // width
    for p in range(parts):
        grads[p * depth : (p + 1) * depth, :] = wh_acc[:, p * width : (p + 1) * width].astype(BF16)
    grads[parts * depth :, :] = wo_acc[...].T.astype(BF16)

    def feat_grad(v):
        @pl.loop(0, points // block)
        def _(i):
            rows = rows_of(i, block)
            out_feats[v][rows, :] = dot(grad_norm[v, rows, :], w_hidden[...], NT).astype(BF16)

    span, rows = half.shape[0], chunk.shape[0]
    z, c = w // 2, lax.rem(w, 2)
    partner = (2 * z + 1 - c, n)
    mine = pl.multiple_of(c * span, span)
    other = pl.multiple_of((1 - c) * span, span)
    swap = remote(grads.at[pl.ds(other, span)], half, sem_pair, 0, partner)
    swap.start()
    swap.wait()
    own[...] = (
        grads[pl.ds(mine, span), :].astype(F32) + half[...].astype(F32)
    ).astype(BF16)

    def to_piece(d):
        return remote(
            own.at[rows_of(lax.rem(n + d, n_narrow), rows)], piece.at[n], sem_piece, d, peer(d)
        )

    start_all(to_piece, n_narrow)
    piece[n] = own[rows_of(n, rows), :]
    feat_grad(0)
    wait_all(to_piece, n_narrow)
    chunk[...] = jnp.sum(piece[...].astype(F32), axis=0).astype(BF16)

    def to_stack(d):
        return remote(
            chunk, stack_in.at[z], sem_stack, d, (2 * lax.rem(z + d, n_z) + c, n)
        )

    start_all(to_stack, n_z)
    stack_in[z] = chunk[...]
    wait_all(to_stack, n_z)
    place = pl.ds(pl.multiple_of(mine + n * rows, rows), rows)
    merged[place, :] = jnp.sum(stack_in[...].astype(F32), axis=0).astype(BF16)

    def to_gather(d):
        return remote(merged.at[place], merged.at[place], sem_gather, d, peer(d))

    start_all(to_gather, n_narrow)
    feat_grad(1)
    wait_all(to_gather, n_narrow)
    swap = remote(merged.at[pl.ds(mine, span)], merged.at[pl.ds(mine, span)], sem_pair, 1, partner)
    swap.start()
    swap.wait()
    for p in range(parts):
        grad_wh_o[:, p * width : (p + 1) * width] = merged[
            p * depth : (p + 1) * depth, :
        ].astype(F32)
    grad_wo_o[...] = merged[parts * depth :, :].astype(F32)


def body(feat_a, feat_b, w_hidden, w_out, send_rows, dest_rows, counts, neg_rows):
    points, depth = feat_a.shape[2:]
    hidden, width = w_out.shape
    n_wide, n_narrow = lax.axis_size("wide"), lax.axis_size("narrow")
    n_z = n_wide // 2
    cap = send_rows.shape[3]
    neg_count = neg_rows.shape[2]
    total_negs = n_narrow * neg_count
    all_points = float(n_wide * n_narrow * points)
    send_row = send_rows.reshape(n_narrow, cap)
    dests = dest_rows.reshape(n_narrow, 1, cap)
    count = jnp.broadcast_to(counts.reshape(n_narrow, 1, 1), (n_narrow, 7, cap))
    msg = jnp.concatenate([dests, count], axis=1)
    stat = (8, hidden)
    grad_total = depth * hidden // width + hidden
    span = grad_total // 2
    rows = span // n_narrow
    vmem = pl.BlockSpec(memory_space=pltpu.VMEM)
    dma = pltpu.SemaphoreType.DMA
    out_shape = (
        jax.ShapeDtypeStruct((8, cap), F32),
        jax.ShapeDtypeStruct((points, depth), BF16),
        jax.ShapeDtypeStruct((points, depth), BF16),
        jax.ShapeDtypeStruct((depth, hidden), F32),
        jax.ShapeDtypeStruct((hidden, width), F32),
    )
    scratch = [
        pltpu.VMEM((2, points, hidden), F32),
        pltpu.VMEM((2, points, hidden), BF16),
        pltpu.VMEM((2, points, width), BF16),
        pltpu.VMEM((2, points, 1), F32),
        pltpu.VMEM((4, 8, hidden), F32),
        pltpu.VMEM(stat, F32),
        pltpu.VMEM((n_narrow,) + stat, F32),
        pltpu.VMEM(stat, F32),
        pltpu.VMEM((n_wide,) + stat, F32),
        pltpu.VMEM(stat, F32),
        pltpu.VMEM((n_narrow,) + stat, F32),
        pltpu.VMEM(stat, F32),
        pltpu.VMEM((n_wide,) + stat, F32),
        pltpu.VMEM(stat, F32),
        pltpu.VMEM((n_narrow, 8, cap), jnp.int32),
        pltpu.VMEM((n_narrow, cap), jnp.int32),
        pltpu.VMEM((points, 1), jnp.int32),
        pltpu.VMEM((total_negs, width), BF16),
        pltpu.VMEM((points, width), BF16),
        pltpu.VMEM((points, width), BF16),
        pltpu.VMEM((points, total_negs), BF16),
        pltpu.VMEM((points, 1), F32),
        pltpu.VMEM((points, width), F32),
        pltpu.VMEM((width, points), BF16),
        pltpu.VMEM((points, width), BF16),
        pltpu.VMEM((points, width), BF16),
        pltpu.VMEM((points, width), BF16),
        pltpu.VMEM((n_narrow, neg_count, width), BF16),
        pltpu.VMEM((n_narrow, neg_count, width), BF16),
        pltpu.VMEM((neg_count, width), BF16),
        pltpu.VMEM((2, points, hidden), BF16),
        pltpu.VMEM((width, hidden), F32),
        pltpu.VMEM((depth, hidden), F32),
        pltpu.VMEM((8, cap), F32),
        pltpu.VMEM((grad_total, width), BF16),
        pltpu.VMEM((span, width), BF16),
        pltpu.VMEM((span, width), BF16),
        pltpu.VMEM((n_narrow, rows, width), BF16),
        pltpu.VMEM((rows, width), BF16),
        pltpu.VMEM((n_z, rows, width), BF16),
        pltpu.VMEM((grad_total, width), BF16),
        dma((2, n_narrow)),
        dma((2, n_narrow)),
        dma((2, n_wide)),
        dma((2, n_narrow)),
        dma((2, n_wide)),
        dma((2, n_narrow)),
        dma((2, n_narrow)),
        dma((2, n_narrow)),
        dma((2, n_narrow)),
        dma((2, 2)),
        dma((2, n_narrow)),
        dma((2, n_z)),
        dma((2, n_narrow)),
    ]
    loss, grad_a, grad_b, grad_wh, grad_wo = pl.pallas_call(
        functools.partial(step_kernel, all_points),
        out_shape=out_shape,
        in_specs=[vmem] * 9,
        out_specs=(vmem,) * 5,
        scratch_shapes=scratch,
        compiler_params=pltpu.CompilerParams(
            collective_id=1, has_side_effects=True, vmem_limit_bytes=63 * 1024 * 1024
        ),
        name="step",
    )(
        feat_a.reshape(points, depth),
        feat_b.reshape(points, depth),
        w_hidden,
        w_out,
        send_row.reshape(points, 1),
        send_row,
        msg,
        neg_rows.reshape(neg_count, 1),
        neg_rows.reshape(1, neg_count),
    )
    return (
        loss[0, 0],
        grad_a.reshape(feat_a.shape),
        grad_b.reshape(feat_b.shape),
        grad_wh,
        grad_wo,
    )


def solution(mesh):
    placed = (
        P("wide", "narrow", None, None),
        P("wide", "narrow", None, None),
        P(),
        P(),
        P("wide", "narrow", None, None),
        P("wide", "narrow", None, None),
        P("wide", "narrow", None),
        P("wide", "narrow", None),
    )
    return jax.shard_map(
        body,
        mesh=mesh,
        in_specs=placed,
        out_specs=(P(), P("wide", "narrow", None, None), P("wide", "narrow", None, None), P(), P()),
        check_vma=False,
    )
```

time: 516 us -> 153 us (0.30)
  waiting for transfers between devices: 172 us -> 0 us
  Pallas kernels: 0 us -> 138 us
  blocking collectives: 136 us -> 0 us
  matrix products: 57.2 us -> 0 us
  other arithmetic: 58.1 us -> 1.35 us
  local copies, waits for them, and re-layouts: 51.1 us -> 12.7 us
  starting transfers between devices: 21.6 us -> 0 us
  between operations: 17.9 us -> 0.65 us
    pallas_call x0 -> x1, Pallas kernels: none -> 138 us  [body(): pl.pallas_call(functools.partial(step_kernel, all_points), out_shape=out_...]
    psum x1 -> x0, waiting for transfers between devices: 137 us -> none  [body(): grad_wh, grad_wo = lax.psum((wh_a + wh_b, wo_a + wo_b), ('wide', 'narrow'))]
    psum x2 -> x0, blocking collectives: 136 us -> none  [the longest x1 68.9 us: body(): lax.psum((moments[0], moments[1], moments[2], moments[3]), ('wide', 'narr...]
    dot_general x18 -> x0, matrix products: 57.2 us -> none  [the longest x2 10.4 us: pair_terms(): lax.dot_general(neg_weight, probe_entry_count, (((0,), (0,)), ((), ())),...]
    scatter-add x3 -> x0, other arithmetic: 29.4 us -> none  [the longest x1 13.4 us: body(): jax.ops.segment_sum(grad_query, dest_flat, num_segments=points)]
    reduce_scatter x1 -> x0, waiting for transfers between devices: 23.6 us -> none  [body(): lax.psum_scatter(grad_neg.astype(jnp.bfloat16), 'narrow', scatter_dimensi...]
    all_to_all x4 -> x0, starting transfers between devices: 21.1 us -> none  [the longest x1 6.67 us: body(): lax.all_to_all(keys_out, 'narrow', split_axis=0, concat_axis=0, tiled=True)]
    gather x3 -> x0, local copies, waits for them, and re-layouts: 19.5 us -> none  [the longest x1 9.06 us: body(): probe_entry_count = embed_a[dest_flat]]
  transfers between devices with their start and end apart: 7 -> 0, of which waited for: 5 -> 0; matrix products, arithmetic and copies ran while one was open for 14% -> 0% of each run, Pallas kernels for 0% -> 0%
where the time goes in v2:
time: 153 us; the launch traced here: 152 us
  Pallas kernels  138 us (90%)
  local copies, waits for them, and re-layouts  12.7 us (8%)
    pallas_call x1, Pallas kernels, body(): pl.pallas_call(functools.partial(step_kernel, all_points), out_shape=out_...  138 us
    unnamed x10, local copies, waits for them, and re-layouts  7.34 us

profile of v2, /device:TPU:1, one launch (start us, length us, event | category | flops | bytes accessed | tf_op | source)
XLA Modules:
  0.0 152.3 jit_solution(4975501946298718010)
XLA Ops:
  0.6 0.7 broadcast_in_dim.8
  1.4 1.4 pad_add_fusion.msg
  2.7 1.4 copy.15.neg_col
  4.1 2.0 %copy.14.send_col = s32[2048,1]{1,0:T(8,128)} copy(s32[2048,1]{0,1:T(1,128)} %bitcast.15) | data formatting | bytes 16384 | tf_op jit(solution)/shard_map/reshape;reshape | solution.py:572
  6.1 137.7 %step.1 = (f32[8,128]{1,0:T(8,128)}, bf16[2048,512]{1,0:T(8,128)(2,1)}, bf16[2048,512]{1,0:T(8,128)(2,1)}, f32[512,512]{1,0:T(8,128)}, f32[512,256]{1,0:T(8,128)}) custom-call(bf16[2048,512]{1,0:T(8,128)(2,1)} %bitcast.11, bf16[2048,512]{1,0:T(8,128)(2,1)} %bitcast.12, bf16[512,512]{1,0:T(8,128)(2,1)} %w_hidden.1, bf16[512,256]{1,0:T(8,128)(2,1)} %w_out.1, ...), custom_call_target="tpu_custom_call" | custom-call | tf_op jit(solution)/shard_map/step/pallas_call | solution.py:557
  143.8 1.2 slice.3
  145.0 0.0 copy-start
  145.0 3.2 %copy.20 = bf16[1,1,2048,512]{3,2,1,0:T(8,128)(2,1)} copy(bf16[1,1,2048,512]{3,2,1,0:T(8,128)(2,1)} %bitcast.14) | data formatting | bytes 4194304
  148.2 0.0 copy-done
  148.2 0.0 copy-start.1
  148.2 1.3 copy.21
  149.5 0.6 copy-done.1
  150.1 0.0 copy-start.2
  150.2 1.0 copy.22
  151.1 0.4 copy-done.2
  151.5 0.8 copy.23
Async XLA Ops:
  145.0 3.2 %copy-start = (bf16[2048,512]{1,0:T(8,128)(2,1)S(1)}, bf16[2048,512]{1,0:T(8,128)(2,1)}, u32[]{:S(2)}) copy-start(bf16[2048,512]{1,0:T(8,128)(2,1)} %get-tuple-element.12) | copy-start | bytes 6291460
  148.2 2.0 %copy-start.1 = (f32[512,512]{1,0:T(8,128)S(1)}, f32[512,512]{1,0:T(8,128)}, u32[]{:S(2)}) copy-start(f32[512,512]{1,0:T(8,128)} %get-tuple-element.23) | copy-start | bytes 3145732
  150.1 1.4 copy-start.2

commit v3 on v2

v3 whole, which is shorter than its diff:
```python
import functools
import math

import jax
import jax.numpy as jnp
from jax import lax
from jax.experimental import pallas as pl
from jax.experimental.pallas import tpu as pltpu
from jax.sharding import PartitionSpec as P

MESH = pl.DeviceIdType.MESH
F32 = jnp.float32
BF16 = jnp.bfloat16
TEMPERATURE = 0.07
NT = (((1,), (1,)), ((), ()))
TN = (((0,), (0,)), ((), ()))


def dot(left, right, dims=None):
    if dims is None:
        return jnp.dot(left, right, preferred_element_type=F32)
    return lax.dot_general(left, right, dims, preferred_element_type=F32)


def one_hot(mask):
    return jnp.where(mask, 1.0, 0.0).astype(F32)


def fold(values):
    rows, width = values.shape
    return jnp.sum(values.reshape(rows // 8, 8, width), axis=0)


def remote(src, dst, sems, d, device):
    return pltpu.make_async_remote_copy(
        src_ref=src,
        dst_ref=dst,
        send_sem=sems.at[0, d],
        recv_sem=sems.at[1, d],
        device_id=device,
        device_id_type=MESH,
    )


def start_all(make, count):
    @pl.loop(1, count)
    def _(d):
        make(d).start()


def wait_all(make, count):
    @pl.loop(1, count)
    def _(d):
        make(d).wait()


def wait_sent(make, count):
    @pl.loop(1, count)
    def _(d):
        make(d).wait_send()


def step_kernel(
    all_points,
    feat_a,
    feat_b,
    w_hidden,
    w_out,
    send_row,
    dest_own,
    counts,
    neg_row,
    loss_o,
    grad_feat_a,
    grad_feat_b,
    grads_o,
    feat,
    feat_slot,
    lin,
    normed,
    embed,
    scale,
    acc,
    feat_acc,
    stat,
    near,
    part,
    far,
    total,
    stat2,
    near2,
    part2,
    far2,
    total2,
    msg,
    msg_in,
    send_col,
    dest_row,
    dest_col,
    live_col,
    query,
    negs,
    keys_in,
    expo,
    exp_sum,
    num,
    spread,
    grad_query,
    grad_out_slots,
    grad_in_slots,
    neg_out,
    neg_in,
    neg_mine,
    grad_norm,
    wo_acc,
    wh_one,
    wh_two,
    loss_acc,
    grads,
    half,
    own,
    piece,
    chunk,
    stack_in,
    sem_in,
    sem_out,
    sem_msg,
    sem_near,
    sem_far,
    sem_near2,
    sem_far2,
    sem_neg,
    sem_key,
    sem_grad,
    sem_negback,
    sem_pair,
    sem_piece,
    sem_stack,
    sem_gather,
):
    w = lax.axis_index("wide")
    n = lax.axis_index("narrow")
    n_wide = far.shape[0]
    n_narrow = near.shape[0]
    n_z = stack_in.shape[0]
    points, depth = feat_a.shape
    hidden = w_hidden.shape[1]
    width = w_out.shape[1]
    cap = points // n_narrow
    neg_count = neg_row.shape[1]
    block = min(512, points)
    small = min(256, points)
    blocks = points // block
    split = hidden // 2

    def peer(d):
        return (w, lax.rem(n + d, n_narrow))

    def source(d):
        return lax.rem(n + n_narrow - d, n_narrow)

    def across(d):
        return (lax.rem(w + d, n_wide), n)

    def rows_of(i, size):
        return pl.ds(pl.multiple_of(i * size, size), size)

    barrier = pltpu.get_barrier_semaphore()

    @pl.loop(1, n_narrow)
    def _(d):
        pl.semaphore_signal(barrier, inc=1, device_id=peer(d), device_id_type=MESH)

    @pl.loop(1, n_wide)
    def _(d):
        pl.semaphore_signal(barrier, inc=1, device_id=across(d), device_id_type=MESH)

    def load(v, i):
        ref = (feat_a, feat_b)[v]
        rows = rows_of(i, block)
        return pltpu.make_async_copy(ref.at[rows], feat.at[v, rows], sem_in.at[v, i])

    for v in (1, 0):
        for i in range(blocks):
            load(v, i).start()

    acc[...] = jnp.zeros_like(acc)
    feat_acc[...] = jnp.zeros_like(feat_acc)
    for v in (1, 0):

        @pl.loop(0, blocks)
        def _(i):
            load(v, i).wait()
            rows = rows_of(i, block)
            points_in = feat[v, rows, :]
            linear = dot(points_in, w_hidden[...])
            acc[2 * v] += fold(linear)
            acc[2 * v + 1] += fold(linear * linear)
            feat_acc[v] += fold(points_in.astype(F32))

    def put_sums(stat, sums):
        for r in range(4):
            stat[2 * r : 2 * r + 1, 0:split] = sums[r : r + 1, 0:split]
            stat[2 * r + 1 : 2 * r + 2, 0:split] = sums[r : r + 1, split:]

    def get_sum(total, r):
        return jnp.concatenate(
            [total[2 * r : 2 * r + 1, 0:split], total[2 * r + 1 : 2 * r + 2, 0:split]], axis=1
        )

    put_sums(stat, jnp.sum(acc[...], axis=1))

    pl.semaphore_wait(barrier, n_narrow + n_wide - 2)

    def sum_all(stat, near, part, far, total, sem_near, sem_far, between=None, later=None):
        def to_near(d):
            return remote(stat, near.at[n], sem_near, d, peer(d))

        def to_far(d):
            return remote(part, far.at[w], sem_far, d, across(d))

        start_all(to_near, n_narrow)
        near[n] = stat[...]
        if between is not None:
            between()
        wait_all(to_near, n_narrow)
        part[...] = jnp.sum(near[...], axis=0)
        start_all(to_far, n_wide)
        far[w] = part[...]
        if later is not None:
            later()
        wait_all(to_far, n_wide)
        total[...] = jnp.sum(far[...], axis=0)

    def to_msg(d):
        return remote(msg.at[lax.rem(n + d, n_narrow)], msg_in.at[n], sem_msg, d, peer(d))

    def gather(ids, table, i):
        lanes = lax.broadcasted_iota(jnp.int32, (block, points), 1)
        return dot(one_hot(ids[rows_of(i, block), :] == lanes).astype(BF16), table)

    def columns(ids, ref):
        square = jnp.concatenate(
            [ids.astype(F32), jnp.zeros((cap - n_narrow, cap), F32)], axis=0
        ).T.astype(jnp.int32)
        for s in range(n_narrow):
            ref[s * cap : (s + 1) * cap, :] = square[:, s : s + 1]

    def spread_counts():
        across_lanes = lax.broadcasted_iota(jnp.int32, (n_narrow, n_narrow), 1)
        down = lax.broadcasted_iota(jnp.int32, (n_narrow, n_narrow), 0)
        here = jnp.broadcast_to(counts[...], (n_narrow, n_narrow)).astype(F32)
        return jnp.sum(jnp.where(across_lanes == down, here, 0.0), axis=1, keepdims=True)

    def slot_order():
        count = spread_counts().astype(jnp.int32)
        line = lax.broadcasted_iota(jnp.int32, (8, cap), 0)
        for s in range(n_narrow):
            msg[s] = jnp.where(line == 0, dest_own[s : s + 1, :], count[s : s + 1, :])
        start_all(to_msg, n_narrow)
        msg_in[n] = msg[n]
        columns(send_row[...], send_col)

        @pl.loop(0, blocks)
        def _(i):
            feat_slot[rows_of(i, block), :] = gather(send_col, feat[1], i).astype(BF16)

    def slot_linear():
        @pl.loop(0, blocks)
        def _(i):
            rows = rows_of(i, block)
            lin[rows, :] = dot(feat_slot[rows, :], w_hidden[...])

        wait_all(to_msg, n_narrow)
        ids = msg_in[:, 0, :]
        dest_row[...] = ids
        columns(ids, dest_col)
        line = lax.broadcasted_iota(jnp.int32, (cap, 1), 0)
        for s in range(n_narrow):
            live_col[s * cap : (s + 1) * cap, :] = one_hot(line < msg_in[s, 1:2, 0:1])

    sum_all(stat, near, part, far, total, sem_near, sem_far, slot_order, slot_linear)

    inv_count = 1.0 / all_points
    means, inverses = [], []
    for v in range(2):
        mean = get_sum(total, 2 * v) * inv_count
        square = get_sum(total, 2 * v + 1) * inv_count
        means.append(mean)
        inverses.append(lax.rsqrt(square - mean * mean + 1e-5))

    def finish(v):
        @pl.loop(0, blocks)
        def _(i):
            rows = rows_of(i, block)
            linear = lin[rows, :] if v else dot(feat[0, rows, :], w_hidden[...])
            value = ((linear - means[v]) * inverses[v]).astype(BF16)
            normed[v, rows, :] = value
            out = dot(jnp.maximum(value, 0), w_out[...])
            unit_scale = lax.rsqrt(jnp.sum(out * out, axis=1, keepdims=True) + 1e-6)
            embed[v, rows, :] = (out * unit_scale).astype(BF16)
            scale[v, rows, :] = unit_scale

    finish(1)
    neg_col = jnp.broadcast_to(neg_row[...].astype(F32), (cap, neg_count)).T.astype(jnp.int32)
    my_negs = rows_of(n, neg_count)
    picks = [
        one_hot(send_row[s : s + 1, :] == neg_col).astype(BF16) for s in range(n_narrow)
    ]
    negs[my_negs, :] = dot(jnp.concatenate(picks, axis=1), embed[1]).astype(BF16)

    def to_negs(d):
        return remote(negs.at[my_negs], negs.at[my_negs], sem_neg, d, peer(d))

    start_all(to_negs, n_narrow)

    def to_key(d):
        return remote(
            embed.at[1, rows_of(lax.rem(n + d, n_narrow), cap)],
            keys_in.at[rows_of(n, cap)],
            sem_key,
            d,
            peer(d),
        )

    start_all(to_key, n_narrow)
    keys_in[rows_of(n, cap), :] = embed[1, rows_of(n, cap), :]

    finish(0)

    @pl.loop(0, blocks)
    def _(i):
        query[rows_of(i, block), :] = gather(dest_col, embed[0], i).astype(BF16)

    wait_all(to_negs, n_narrow)

    to_exp2 = math.log2(math.e) / TEMPERATURE

    @pl.loop(0, points // small)
    def _(i):
        rows = rows_of(i, small)
        score = dot(query[rows, :], negs[...], NT)
        power = jnp.exp2(score * to_exp2)
        exp_sum[rows, :] = jnp.sum(power, axis=1, keepdims=True)
        power = power.astype(BF16)
        expo[rows, :] = power
        num[rows, :] = dot(power, negs[...])

    wh_two[...] = jnp.zeros_like(wh_two)
    wh_one[...] = jnp.zeros_like(wh_one)

    def view_rows(v, rows):
        return feat_slot[rows, :] if v else feat[0, rows, :]

    for v in range(2):

        @pl.loop(0, blocks)
        def _(i):
            rows = rows_of(i, block)
            wh_two[v] += dot(view_rows(v, rows), normed[v, rows, :], TN)

    loss_acc[...] = jnp.zeros_like(loss_acc)

    def to_slot(d):
        rows = rows_of(source(d), cap)
        return remote(
            grad_out_slots.at[rows],
            grad_in_slots.at[rows_of(n, cap)],
            sem_grad,
            d,
            (w, source(d)),
        )

    @pl.loop(0, n_narrow)
    def _(d):
        @pl.when(d > 0)
        def _():
            to_key(d).wait_recv()

        rows = rows_of(source(d), cap)
        live = live_col[rows, :]
        key = keys_in[rows, :].astype(F32)
        asked = query[rows, :].astype(F32)
        positive = jnp.sum(asked * key, axis=1, keepdims=True) * (1.0 / TEMPERATURE)
        exp_pos = jnp.exp(positive)
        denominator = exp_pos + exp_sum[rows, :]
        term = live * (jnp.log(denominator) - positive)
        loss_acc[...] += jnp.sum(term, axis=0, keepdims=True)
        weight = live * (1.0 / TEMPERATURE)
        share = weight / denominator
        pair_coeff = share * exp_pos - weight
        grad_out_slots[rows, :] = (pair_coeff * asked).astype(BF16)

        @pl.when(d > 0)
        def _():
            to_slot(d).start()

        grad_query[rows, :] = (pair_coeff * key + share * num[rows, :]).astype(BF16)
        spread[:, rows] = (share * asked).T.astype(BF16)

    grad_in_slots[rows_of(n, cap), :] = grad_out_slots[rows_of(n, cap), :]

    def to_owner(d):
        return remote(
            neg_out.at[rows_of(lax.rem(n + d, n_narrow), neg_count)],
            neg_in.at[n],
            sem_negback,
            d,
            peer(d),
        )

    batch = min(4, n_narrow)
    batches = n_narrow // batch

    @pl.loop(0, batches)
    def _(i):
        q = lax.rem(n // batch + i, batches)
        cols = rows_of(q, batch * neg_count)
        neg_out[cols, :] = dot(spread[...], expo[:, cols]).T.astype(BF16)
        for k in range(batch):
            d = lax.rem(q * batch + k - n + n_narrow, n_narrow)

            @pl.when(d > 0)
            def _():
                to_owner(d).start()

    neg_in[n] = neg_out[rows_of(n, neg_count), :]

    def rows_one_hot(row_ids, i, size):
        place = lax.broadcasted_iota(jnp.int32, (size, cap), 0) + i * size
        picks = [
            one_hot(row_ids[s : s + 1, :] == place).astype(BF16) for s in range(n_narrow)
        ]
        return jnp.concatenate(picks, axis=1)

    acc[...] = jnp.zeros_like(acc)
    wo_acc[...] = jnp.zeros_like(wo_acc)

    def back_top(v, grad_embed):
        @pl.loop(0, blocks)
        def _(i):
            rows = rows_of(i, block)
            grad = grad_embed(i, rows)
            unit = embed[v, rows, :].astype(F32)
            inner = jnp.sum(unit * grad, axis=1, keepdims=True)
            grad_out = (scale[v, rows, :] * (grad - unit * inner)).astype(BF16)
            value = normed[v, rows, :]
            wo_acc[...] += dot(grad_out, jnp.maximum(value, 0), TN)
            value = value.astype(F32)
            grad_act = jnp.where(value > 0, dot(grad_out, w_out[...], NT), 0.0)
            acc[2 * v] += fold(grad_act)
            acc[2 * v + 1] += fold(grad_act * value)
            grad_norm[v, rows, :] = grad_act.astype(BF16)

    def first_product(v):
        @pl.loop(0, blocks)
        def _(i):
            rows = rows_of(i, block)
            wh_one[v] += dot(view_rows(v, rows), grad_norm[v, rows, :], TN)

    back_top(0, lambda i, rows: dot(rows_one_hot(dest_row, i, block), grad_query[...]))
    first_product(0)

    wait_sent(to_key, n_narrow)
    wait_all(to_slot, n_narrow)
    wait_all(to_owner, n_narrow)
    neg_mine[...] = jnp.sum(neg_in[...].astype(F32), axis=0).astype(BF16)

    def grad_b(i, rows):
        mask = one_hot(send_col[rows, :] == neg_row[...]).astype(BF16)
        return grad_in_slots[rows, :].astype(F32) + dot(mask, neg_mine[...])

    back_top(1, grad_b)

    put_sums(stat2, jnp.sum(acc[...], axis=1))
    stat2[0:1, split:] = loss_acc[0:1, :]
    stat2[1:8, split:] = jnp.broadcast_to(
        jnp.sum(spread_counts(), axis=0, keepdims=True), (7, cap)
    )
    sum_all(
        stat2,
        near2,
        part2,
        far2,
        total2,
        sem_near2,
        sem_far2,
        lambda: first_product(1),
    )

    pair_total = total2[1:2, split : split + 1]
    grad_weight = all_points / pair_total
    loss_o[...] = jnp.broadcast_to(total2[0:1, split:] / pair_total, loss_o.shape)
    mean_grads = [get_sum(total2, 2 * v) * inv_count for v in range(2)]
    mean_crosses = [get_sum(total2, 2 * v + 1) * inv_count for v in range(2)]
    scales = [inverses[v] * grad_weight for v in range(2)]
    parts = hidden // width
    totals = [jnp.sum(feat_acc[v], axis=0, keepdims=True) for v in range(2)]
    downs = [jnp.broadcast_to(row, (8, depth)).T[:, 0:1] for row in totals]
    for p in range(parts):
        cols = slice(p * width, (p + 1) * width)
        value = sum(
            scales[v][:, cols]
            * (
                wh_one[v, :, cols]
                - downs[v] * mean_grads[v][:, cols]
                - wh_two[v, :, cols] * mean_crosses[v][:, cols]
            )
            for v in range(2)
        )
        grads[p * depth : (p + 1) * depth, :] = value.astype(BF16)
    grads[parts * depth :, :] = (wo_acc[...].T * grad_weight).astype(BF16)

    def store(v, i):
        ref = (grad_feat_a, grad_feat_b)[v]
        rows = rows_of(i, block)
        return pltpu.make_async_copy(normed.at[v, rows], ref.at[rows], sem_out.at[v, i])

    def feat_grad(v):
        @pl.loop(0, blocks)
        def _(i):
            rows = rows_of(i, block)
            grad = grad_norm[v, rows, :].astype(F32)
            value = normed[v, rows, :].astype(F32)
            grad = scales[v] * (grad - mean_grads[v] - value * mean_crosses[v])
            out = dot(grad.astype(BF16), w_hidden[...], NT).astype(BF16)
            if v:
                feat_slot[rows, :] = out
            else:
                normed[v, rows, :] = out
                store(v, i).start()

    def row_order():
        @pl.loop(0, blocks)
        def _(i):
            picks = rows_one_hot(send_row, i, block)
            normed[1, rows_of(i, block), :] = dot(picks, feat_slot[...]).astype(BF16)
            store(1, i).start()

    span, rows = half.shape[0], chunk.shape[0]
    z, c = w // 2, lax.rem(w, 2)
    partner = (2 * z + 1 - c, n)
    mine = pl.multiple_of(c * span, span)
    other = pl.multiple_of((1 - c) * span, span)
    swap = remote(grads.at[pl.ds(other, span)], half, sem_pair, 0, partner)
    swap.start()
    swap.wait()
    own[...] = (
        grads[pl.ds(mine, span), :].astype(F32) + half[...].astype(F32)
    ).astype(BF16)

    def to_piece(d):
        return remote(
            own.at[rows_of(lax.rem(n + d, n_narrow), rows)], piece.at[n], sem_piece, d, peer(d)
        )

    start_all(to_piece, n_narrow)
    piece[n] = own[rows_of(n, rows), :]
    feat_grad(0)
    wait_all(to_piece, n_narrow)
    chunk[...] = jnp.sum(piece[...].astype(F32), axis=0).astype(BF16)

    def to_stack(d):
        return remote(
            chunk, stack_in.at[z], sem_stack, d, (2 * lax.rem(z + d, n_z) + c, n)
        )

    start_all(to_stack, n_z)
    stack_in[z] = chunk[...]
    feat_grad(1)
    wait_all(to_stack, n_z)
    place = pl.ds(pl.multiple_of(mine + n * rows, rows), rows)
    grads_o[place, :] = jnp.sum(stack_in[...].astype(F32), axis=0).astype(BF16)

    def to_gather(d):
        return remote(grads_o.at[place], grads_o.at[place], sem_gather, d, peer(d))

    start_all(to_gather, n_narrow)
    row_order()
    wait_all(to_gather, n_narrow)
    swap = remote(
        grads_o.at[pl.ds(mine, span)], grads_o.at[pl.ds(mine, span)], sem_pair, 1, partner
    )
    swap.start()
    for v in range(2):
        for i in range(blocks):
            store(v, i).wait()
    swap.wait()


def deliver_kernel(loss, grad_a, grad_b, grads, loss_o, out_a, out_b, out_wh, out_wo, sems):
    pieces = sems.shape[1]
    rows = grad_a.shape[0] // pieces
    copies = [
        pltpu.make_async_copy(
            src.at[pl.ds(i * rows, rows)], dst.at[pl.ds(i * rows, rows)], sems.at[v, i]
        )
        for v, (src, dst) in enumerate(((grad_a, out_a), (grad_b, out_b)))
        for i in range(pieces)
    ]
    for copy in copies:
        copy.start()
    depth, hidden = out_wh.shape
    width = out_wo.shape[1]
    for p in range(hidden // width):
        out_wh[:, p * width : (p + 1) * width] = grads[p * depth : (p + 1) * depth, :].astype(F32)
    out_wo[...] = grads[hidden // width * depth :, :].astype(F32)
    loss_o[...] = loss[0:1, 0:1]
    for copy in copies:
        copy.wait()


def body(feat_a, feat_b, w_hidden, w_out, send_rows, dest_rows, counts, neg_rows):
    points, depth = feat_a.shape[2:]
    hidden, width = w_out.shape
    n_wide, n_narrow = lax.axis_size("wide"), lax.axis_size("narrow")
    n_z = n_wide // 2
    cap = send_rows.shape[3]
    neg_count = neg_rows.shape[2]
    total_negs = n_narrow * neg_count
    all_points = float(n_wide * n_narrow * points)
    blocks = points // min(512, points)
    stat = (8, hidden // 2)
    stat2 = (8, hidden // 2 + cap)
    grad_total = depth * hidden // width + hidden
    span = grad_total // 2
    rows = span // n_narrow
    vmem = pl.BlockSpec(memory_space=pltpu.VMEM)
    anywhere = pl.BlockSpec(memory_space=pl.ANY)
    dma = pltpu.SemaphoreType.DMA
    out_shape = (
        jax.ShapeDtypeStruct((8, cap), F32),
        jax.ShapeDtypeStruct((points, depth), BF16),
        jax.ShapeDtypeStruct((points, depth), BF16),
        jax.ShapeDtypeStruct((grad_total, width), BF16),
    )
    scratch = [
        pltpu.VMEM((2, points, depth), BF16),
        pltpu.VMEM((points, depth), BF16),
        pltpu.VMEM((points, hidden), F32),
        pltpu.VMEM((2, points, hidden), BF16),
        pltpu.VMEM((2, points, width), BF16),
        pltpu.VMEM((2, points, 1), F32),
        pltpu.VMEM((4, 8, hidden), F32),
        pltpu.VMEM((2, 8, depth), F32),
        pltpu.VMEM(stat, F32),
        pltpu.VMEM((n_narrow,) + stat, F32),
        pltpu.VMEM(stat, F32),
        pltpu.VMEM((n_wide,) + stat, F32),
        pltpu.VMEM(stat, F32),
        pltpu.VMEM(stat2, F32),
        pltpu.VMEM((n_narrow,) + stat2, F32),
        pltpu.VMEM(stat2, F32),
        pltpu.VMEM((n_wide,) + stat2, F32),
        pltpu.VMEM(stat2, F32),
        pltpu.VMEM((n_narrow, 8, cap), jnp.int32),
        pltpu.VMEM((n_narrow, 8, cap), jnp.int32),
        pltpu.VMEM((points, 1), jnp.int32),
        pltpu.VMEM((n_narrow, cap), jnp.int32),
        pltpu.VMEM((points, 1), jnp.int32),
        pltpu.VMEM((points, 1), F32),
        pltpu.VMEM((points, width), BF16),
        pltpu.VMEM((total_negs, width), BF16),
        pltpu.VMEM((points, width), BF16),
        pltpu.VMEM((points, total_negs), BF16),
        pltpu.VMEM((points, 1), F32),
        pltpu.VMEM((points, width), F32),
        pltpu.VMEM((width, points), BF16),
        pltpu.VMEM((points, width), BF16),
        pltpu.VMEM((points, width), BF16),
        pltpu.VMEM((points, width), BF16),
        pltpu.VMEM((total_negs, width), BF16),
        pltpu.VMEM((n_narrow, neg_count, width), BF16),
        pltpu.VMEM((neg_count, width), BF16),
        pltpu.VMEM((2, points, hidden), BF16),
        pltpu.VMEM((width, hidden), F32),
        pltpu.VMEM((2, depth, hidden), F32),
        pltpu.VMEM((2, depth, hidden), F32),
        pltpu.VMEM((8, cap), F32),
        pltpu.VMEM((grad_total, width), BF16),
        pltpu.VMEM((span, width), BF16),
        pltpu.VMEM((span, width), BF16),
        pltpu.VMEM((n_narrow, rows, width), BF16),
        pltpu.VMEM((rows, width), BF16),
        pltpu.VMEM((n_z, rows, width), BF16),
        dma((2, blocks)),
        dma((2, blocks)),
        dma((2, n_narrow)),
        dma((2, n_narrow)),
        dma((2, n_wide)),
        dma((2, n_narrow)),
        dma((2, n_wide)),
        dma((2, n_narrow)),
        dma((2, n_narrow)),
        dma((2, n_narrow)),
        dma((2, n_narrow)),
        dma((2, 2)),
        dma((2, n_narrow)),
        dma((2, n_z)),
        dma((2, n_narrow)),
    ]
    loss, grad_a, grad_b, grads = pl.pallas_call(
        functools.partial(step_kernel, all_points),
        out_shape=out_shape,
        in_specs=[anywhere] * 2 + [vmem] * 6,
        out_specs=(vmem, anywhere, anywhere, vmem),
        scratch_shapes=scratch,
        compiler_params=pltpu.CompilerParams(
            collective_id=1, has_side_effects=True, vmem_limit_bytes=63 * 1024 * 1024
        ),
        name="step",
    )(
        feat_a.reshape(points, depth),
        feat_b.reshape(points, depth),
        w_hidden,
        w_out,
        send_rows.reshape(n_narrow, cap),
        dest_rows.reshape(n_narrow, cap),
        counts.reshape(1, n_narrow),
        neg_rows.reshape(1, neg_count),
    )
    loss, grad_a, grad_b, grad_wh, grad_wo = pl.pallas_call(
        deliver_kernel,
        out_shape=(
            jax.ShapeDtypeStruct((1, 1), F32),
            jax.ShapeDtypeStruct((points, depth), BF16),
            jax.ShapeDtypeStruct((points, depth), BF16),
            jax.ShapeDtypeStruct((depth, hidden), F32),
            jax.ShapeDtypeStruct((hidden, width), F32),
        ),
        in_specs=[vmem, anywhere, anywhere, vmem],
        out_specs=(vmem, anywhere, anywhere, vmem, vmem),
        scratch_shapes=[dma((2, 4))],
        compiler_params=pltpu.CompilerParams(vmem_limit_bytes=16 * 1024 * 1024),
        name="deliver",
    )(loss, grad_a, grad_b, grads)
    return (
        loss.reshape(()),
        grad_a.reshape(feat_a.shape),
        grad_b.reshape(feat_b.shape),
        grad_wh,
        grad_wo,
    )


def solution(mesh):
    placed = (
        P("wide", "narrow", None, None),
        P("wide", "narrow", None, None),
        P(),
        P(),
        P("wide", "narrow", None, None),
        P("wide", "narrow", None, None),
        P("wide", "narrow", None),
        P("wide", "narrow", None),
    )
    return jax.shard_map(
        body,
        mesh=mesh,
        in_specs=placed,
        out_specs=(P(), P("wide", "narrow", None, None), P("wide", "narrow", None, None), P(), P()),
        check_vma=False,
    )
```

time: 153 us -> 135 us (0.88)
  Pallas kernels: 138 us -> 129 us
  local copies, waits for them, and re-layouts: 12.7 us -> 4.98 us
    pallas_call x1, Pallas kernels: 138 us -> 126 us  [body(): pl.pallas_call(functools.partial(step_kernel, all_points), out_shape=out_...]
    pallas_call x0 -> x1, Pallas kernels: none -> 3.21 us  [body(): pl.pallas_call(deliver_kernel, out_shape=(jax.ShapeDtypeStruct((1, 1), F3...]
    unnamed x10 -> x8, local copies, waits for them, and re-layouts: 7.34 us -> 4.98 us
    another operation x1 -> x0, local copies, waits for them, and re-layouts: 2.04 us -> none  [body(): send_row.reshape(points, 1)]
where the time goes in v3:
time: 135 us
  Pallas kernels  129 us (96%)
  local copies, waits for them, and re-layouts  4.98 us (4%)
    pallas_call x1, Pallas kernels, body(): pl.pallas_call(functools.partial(step_kernel, all_points), out_shape=out_...  126 us
    unnamed x8, local copies, waits for them, and re-layouts  4.98 us
    pallas_call x1, Pallas kernels, body(): pl.pallas_call(deliver_kernel, out_shape=(jax.ShapeDtypeStruct((1, 1), F3...  3.21 us

profile of v3, /device:TPU:1, one launch (start us, length us, event | category | flops | bytes accessed | tf_op | source)
XLA Modules:
  0.0 134.7 jit_solution(5083661893371110958)
XLA Ops:
  0.6 125.9 %step.1 = (f32[8,128]{1,0:T(8,128)}, bf16[2048,512]{1,0:T(8,128)(2,1)}, bf16[2048,512]{1,0:T(8,128)(2,1)}, bf16[1536,256]{1,0:T(8,128)(2,1)}) custom-call(bf16[2048,512]{1,0:T(8,128)(2,1)} %bitcast.9, bf16[2048,512]{1,0:T(8,128)(2,1)} %bitcast.10, bf16[512,512]{1,0:T(8,128)(2,1)} %w_hidden.1, bf16[512,256]{1,0:T(8,128)(2,1)} %w_out.1, s32[16,128]{1,0:T(8,128)} %bitcast.11, ...), custom_call_target="tpu_custom_call" | custom-call | tf_op jit(solution)/shard_map/step/pallas_call | solution.py:702
  126.5 0.0 copy-start
  126.6 1.6 %copy-done = bf16[2048,512]{1,0:T(8,128)(2,1)S(1)} copy-done((bf16[2048,512]{1,0:T(8,128)(2,1)S(1)}, bf16[2048,512]{1,0:T(8,128)(2,1)}, u32[]{:S(2)}) %copy-start) | copy-done | bytes 2097176
  128.1 0.0 copy-start.1
  128.1 1.6 %copy-done.1 = bf16[2048,512]{1,0:T(8,128)(2,1)S(1)} copy-done((bf16[2048,512]{1,0:T(8,128)(2,1)S(1)}, bf16[2048,512]{1,0:T(8,128)(2,1)}, u32[]{:S(2)}) %copy-start.1) | copy-done | bytes 2097176
  129.7 0.0 copy-start.2
  129.7 1.1 copy-done.2
  130.9 0.0 copy-start.3
  130.9 0.7 copy-done.3
  131.5 3.2 %deliver.1 = (f32[1,1]{1,0:T(1,128)}, bf16[2048,512]{1,0:T(8,128)(2,1)}, bf16[2048,512]{1,0:T(8,128)(2,1)}, f32[512,512]{1,0:T(8,128)}, f32[512,256]{1,0:T(8,128)}) custom-call(f32[8,128]{1,0:T(8,128)S(1)} %copy-done.3, bf16[2048,512]{1,0:T(8,128)(2,1)S(1)} %copy-done, bf16[2048,512]{1,0:T(8,128)(2,1)S(1)} %copy-done.1, bf16[1536,256]{1,0:T(8,128)(2,1)S(1)} %copy-done.2), custom_call_target="tpu_custom_call" | custom-call | tf_op jit(solution)/shard_map/deliver/pallas_call | solution.py:722
Async XLA Ops:
  126.5 1.6 %copy-start = (bf16[2048,512]{1,0:T(8,128)(2,1)S(1)}, bf16[2048,512]{1,0:T(8,128)(2,1)}, u32[]{:S(2)}) copy-start(bf16[2048,512]{1,0:T(8,128)(2,1)} %get-tuple-element.15.grad_a) | copy-start | bytes 6291460
  128.1 1.6 %copy-start.1 = (bf16[2048,512]{1,0:T(8,128)(2,1)S(1)}, bf16[2048,512]{1,0:T(8,128)(2,1)}, u32[]{:S(2)}) copy-start(bf16[2048,512]{1,0:T(8,128)(2,1)} %get-tuple-element.16.grad_b) | copy-start | bytes 6291460
  129.7 1.1 copy-start.2
  130.9 0.7 copy-start.3

commit v4 on v3

--- a/solution.py
+++ b/solution.py
@@ -109,7 +109,12 @@
     grad_out_slots,
     grad_in_slots,
     neg_out,
-    neg_in,
+    low_in,
+    high_in,
+    low_mid,
+    high_mid,
+    low_end,
+    high_end,
     neg_mine,
     grad_norm,
     wo_acc,
@@ -152,9 +157,19 @@
     small = min(256, points)
     blocks = points // block
     split = hidden // 2
+    side = negs.shape[0]
+    upper = neg_count // 2
+    row, col = n // side, lax.rem(n, side)
+    halves = (slice(0, upper), slice(upper, neg_count))
 
     def peer(d):
         return (w, lax.rem(n + d, n_narrow))
+
+    def along_row(d):
+        return (w, row * side + lax.rem(col + d, side))
+
+    def along_col(d):
+        return (w, lax.rem(row + d, side) * side + col)
 
     def source(d):
         return lax.rem(n + n_narrow - d, n_narrow)
@@ -303,16 +318,36 @@
 
     finish(1)
     neg_col = jnp.broadcast_to(neg_row[...].astype(F32), (cap, neg_count)).T.astype(jnp.int32)
-    my_negs = rows_of(n, neg_count)
     picks = [
         one_hot(send_row[s : s + 1, :] == neg_col).astype(BF16) for s in range(n_narrow)
     ]
-    negs[my_negs, :] = dot(jnp.concatenate(picks, axis=1), embed[1]).astype(BF16)
-
-    def to_negs(d):
-        return remote(negs.at[my_negs], negs.at[my_negs], sem_neg, d, peer(d))
-
-    start_all(to_negs, n_narrow)
+    negs[row, col] = dot(jnp.concatenate(picks, axis=1), embed[1]).astype(BF16)
+
+    def neg_first(d):
+        low, high = negs.at[row, col, halves[0]], negs.at[row, col, halves[1]]
+        return (
+            remote(low, low, sem_neg, d, along_row(d)),
+            remote(high, high, sem_neg, side + d, along_col(d)),
+        )
+
+    def neg_second(d):
+        low, high = negs.at[row, :, halves[0]], negs.at[:, col, halves[1]]
+        return (
+            remote(low, low, sem_neg, 2 * side + d, along_col(d)),
+            remote(high, high, sem_neg, 3 * side + d, along_row(d)),
+        )
+
+    def start_both(make):
+        for d in range(1, side):
+            for copy in make(d):
+                copy.start()
+
+    def wait_both(make):
+        for d in range(1, side):
+            for copy in make(d):
+                copy.wait()
+
+    start_both(neg_first)
 
     def to_key(d):
         return remote(
@@ -328,23 +363,28 @@
 
     finish(0)
 
+    wait_both(neg_first)
+    start_both(neg_second)
+
     @pl.loop(0, blocks)
     def _(i):
         query[rows_of(i, block), :] = gather(dest_col, embed[0], i).astype(BF16)
 
-    wait_all(to_negs, n_narrow)
+    wait_both(neg_second)
+    total_negs = n_narrow * neg_count
 
     to_exp2 = math.log2(math.e) / TEMPERATURE
 
     @pl.loop(0, points // small)
     def _(i):
         rows = rows_of(i, small)
-        score = dot(query[rows, :], negs[...], NT)
+        table = negs[...].reshape(total_negs, width)
+        score = dot(query[rows, :], table, NT)
         power = jnp.exp2(score * to_exp2)
         exp_sum[rows, :] = jnp.sum(power, axis=1, keepdims=True)
         power = power.astype(BF16)
         expo[rows, :] = power
-        num[rows, :] = dot(power, negs[...])
+        num[rows, :] = dot(power, table)
 
     wh_two[...] = jnp.zeros_like(wh_two)
     wh_one[...] = jnp.zeros_like(wh_one)
@@ -371,12 +411,7 @@
             (w, source(d)),
         )
 
-    @pl.loop(0, n_narrow)
-    def _(d):
-        @pl.when(d > 0)
-        def _():
-            to_key(d).wait_recv()
-
+    def answer(d):
         rows = rows_of(source(d), cap)
         live = live_col[rows, :]
         key = keys_in[rows, :].astype(F32)
@@ -385,46 +420,92 @@
         exp_pos = jnp.exp(positive)
         denominator = exp_pos + exp_sum[rows, :]
         term = live * (jnp.log(denominator) - positive)
-        loss_acc[...] += jnp.sum(term, axis=0, keepdims=True)
         weight = live * (1.0 / TEMPERATURE)
         share = weight / denominator
         pair_coeff = share * exp_pos - weight
         grad_out_slots[rows, :] = (pair_coeff * asked).astype(BF16)
-
-        @pl.when(d > 0)
-        def _():
-            to_slot(d).start()
-
         grad_query[rows, :] = (pair_coeff * key + share * num[rows, :]).astype(BF16)
         spread[:, rows] = (share * asked).T.astype(BF16)
-
-    grad_in_slots[rows_of(n, cap), :] = grad_out_slots[rows_of(n, cap), :]
-
-    def to_owner(d):
-        return remote(
-            neg_out.at[rows_of(lax.rem(n + d, n_narrow), neg_count)],
-            neg_in.at[n],
-            sem_negback,
-            d,
-            peer(d),
-        )
-
-    batch = min(4, n_narrow)
-    batches = n_narrow // batch
-
-    @pl.loop(0, batches)
+        return jnp.sum(term, axis=0, keepdims=True)
+
+    pair = 2
+
+    @pl.loop(0, n_narrow // pair)
     def _(i):
-        q = lax.rem(n // batch + i, batches)
-        cols = rows_of(q, batch * neg_count)
-        neg_out[cols, :] = dot(spread[...], expo[:, cols]).T.astype(BF16)
-        for k in range(batch):
-            d = lax.rem(q * batch + k - n + n_narrow, n_narrow)
+        for k in range(pair):
+            d = i * pair + k
 
             @pl.when(d > 0)
             def _():
-                to_owner(d).start()
-
-    neg_in[n] = neg_out[rows_of(n, neg_count), :]
+                to_key(d).wait_recv()
+
+        loss_acc[...] += sum(answer(i * pair + k) for k in range(pair))
+        for k in range(pair):
+            d = i * pair + k
+
+            @pl.when(d > 0)
+            def _():
+                to_slot(d).start()
+
+    grad_in_slots[rows_of(n, cap), :] = grad_out_slots[rows_of(n, cap), :]
+
+    def to_owner_row(q):
+        d = lax.rem(q - row + side, side)
+        return remote(
+            neg_out.at[q, :, halves[0]], low_in.at[row], sem_negback, d, (w, q * side + col)
+        )
+
+    def to_owner_col(d):
+        q = lax.rem(col + d, side)
+        return remote(
+            neg_out.at[:, q, halves[1]], high_in.at[col], sem_negback, side + d, along_row(d)
+        )
+
+    def to_owner_second(d):
+        return (
+            remote(
+                low_mid.at[lax.rem(col + d, side)],
+                low_end.at[col],
+                sem_negback,
+                2 * side + d,
+                along_row(d),
+            ),
+            remote(
+                high_mid.at[lax.rem(row + d, side)],
+                high_end.at[row],
+                sem_negback,
+                3 * side + d,
+                along_col(d),
+            ),
+        )
+
+    @pl.loop(1, side + 1)
+    def _(i):
+        q = lax.rem(row + i, side)
+        cols = rows_of(q, side * neg_count)
+        neg_out[q] = (
+            dot(spread[...], expo[:, cols]).T.astype(BF16).reshape(side, neg_count, width)
+        )
+
+        @pl.when(i < side)
+        def _():
+            to_owner_row(q).start()
+
+    start_all(to_owner_col, side)
+    low_in[row] = neg_out[row, :, halves[0]]
+    high_in[col] = neg_out[:, col, halves[1]]
+
+    def pass_on():
+        @pl.loop(1, side)
+        def _(i):
+            to_owner_row(lax.rem(row + i, side)).wait()
+
+        wait_all(to_owner_col, side)
+        low_mid[...] = jnp.sum(low_in[...].astype(F32), axis=0).astype(BF16)
+        high_mid[...] = jnp.sum(high_in[...].astype(F32), axis=0).astype(BF16)
+        start_both(to_owner_second)
+        low_end[col] = low_mid[col]
+        high_end[row] = high_mid[row]
 
     def rows_one_hot(row_ids, i, size):
         place = lax.broadcasted_iota(jnp.int32, (size, cap), 0) + i * size
@@ -459,12 +540,14 @@
             wh_one[v] += dot(view_rows(v, rows), grad_norm[v, rows, :], TN)
 
     back_top(0, lambda i, rows: dot(rows_one_hot(dest_row, i, block), grad_query[...]))
+    pass_on()
     first_product(0)
 
     wait_sent(to_key, n_narrow)
     wait_all(to_slot, n_narrow)
-    wait_all(to_owner, n_narrow)
-    neg_mine[...] = jnp.sum(neg_in[...].astype(F32), axis=0).astype(BF16)
+    wait_both(to_owner_second)
+    neg_mine[halves[0], :] = jnp.sum(low_end[...].astype(F32), axis=0).astype(BF16)
+    neg_mine[halves[1], :] = jnp.sum(high_end[...].astype(F32), axis=0).astype(BF16)
 
     def grad_b(i, rows):
         mask = one_hot(send_col[rows, :] == neg_row[...]).astype(BF16)
@@ -615,6 +698,7 @@
     hidden, width = w_out.shape
     n_wide, n_narrow = lax.axis_size("wide"), lax.axis_size("narrow")
     n_z = n_wide // 2
+    side = math.isqrt(n_narrow)
     cap = send_rows.shape[3]
     neg_count = neg_rows.shape[2]
     total_negs = n_narrow * neg_count
@@ -660,7 +744,7 @@
         pltpu.VMEM((points, 1), jnp.int32),
         pltpu.VMEM((points, 1), F32),
         pltpu.VMEM((points, width), BF16),
-        pltpu.VMEM((total_negs, width), BF16),
+        pltpu.VMEM((side, side, neg_count, width), BF16),
         pltpu.VMEM((points, width), BF16),
         pltpu.VMEM((points, total_negs), BF16),
         pltpu.VMEM((points, 1), F32),
@@ -669,8 +753,13 @@
         pltpu.VMEM((points, width), BF16),
         pltpu.VMEM((points, width), BF16),
         pltpu.VMEM((points, width), BF16),
-        pltpu.VMEM((total_negs, width), BF16),
-        pltpu.VMEM((n_narrow, neg_count, width), BF16),
+        pltpu.VMEM((side, side, neg_count, width), BF16),
+        pltpu.VMEM((side, side, neg_count // 2, width), BF16),
+        pltpu.VMEM((side, side, neg_count // 2, width), BF16),
+        pltpu.VMEM((side, neg_count // 2, width), BF16),
+        pltpu.VMEM((side, neg_count // 2, width), BF16),
+        pltpu.VMEM((side, neg_count // 2, width), BF16),
+        pltpu.VMEM((side, neg_count // 2, width), BF16),
         pltpu.VMEM((neg_count, width), BF16),
         pltpu.VMEM((2, points, hidden), BF16),
         pltpu.VMEM((width, hidden), F32),
@@ -690,10 +779,10 @@
         dma((2, n_wide)),
         dma((2, n_narrow)),
         dma((2, n_wide)),
+        dma((2, 4 * side)),
         dma((2, n_narrow)),
         dma((2, n_narrow)),
-        dma((2, n_narrow)),
-        dma((2, n_narrow)),
+        dma((2, 4 * side)),
         dma((2, 2)),
         dma((2, n_narrow)),
         dma((2, n_z)),
@@ -731,7 +820,7 @@
         in_specs=[vmem, anywhere, anywhere, vmem],
         out_specs=(vmem, anywhere, anywhere, vmem, vmem),
         scratch_shapes=[dma((2, 4))],
-        compiler_params=pltpu.CompilerParams(vmem_limit_bytes=16 * 1024 * 1024),
+        compiler_params=pltpu.CompilerParams(vmem_limit_bytes=63 * 1024 * 1024),
         name="deliver",
     )(loss, grad_a, grad_b, grads)
     return (

time: 135 us -> 255 us (1.89)
  Pallas kernels: 129 us -> 254 us
  local copies, waits for them, and re-layouts: 4.98 us -> 0 us
    pallas_call x1, Pallas kernels: 3.21 us -> 131 us  [body(): pl.pallas_call(deliver_kernel, out_shape=(jax.ShapeDtypeStruct((1, 1), F3...]
    unnamed x8 -> x0, local copies, waits for them, and re-layouts: 4.98 us -> none
where the time goes in v4:
time: 255 us
  Pallas kernels  254 us (100%)
    pallas_call x1, Pallas kernels, body(): pl.pallas_call(deliver_kernel, out_shape=(jax.ShapeDtypeStruct((1, 1), F3...  131 us
    pallas_call x1, Pallas kernels, body(): pl.pallas_call(functools.partial(step_kernel, all_points), out_shape=out_...  124 us

profile of v4, /device:TPU:1, one launch (start us, length us, event | category | flops | bytes accessed | tf_op | source)
XLA Modules:
  0.0 254.9 jit_solution(2130188429982274423)
XLA Ops:
  0.6 123.7 %step.1 = (f32[8,128]{1,0:T(8,128)}, bf16[2048,512]{1,0:T(8,128)(2,1)}, bf16[2048,512]{1,0:T(8,128)(2,1)}, bf16[1536,256]{1,0:T(8,128)(2,1)}) custom-call(bf16[2048,512]{1,0:T(8,128)(2,1)} %bitcast.9, bf16[2048,512]{1,0:T(8,128)(2,1)} %bitcast.10, bf16[512,512]{1,0:T(8,128)(2,1)} %w_hidden.1, bf16[512,256]{1,0:T(8,128)(2,1)} %w_out.1, s32[16,128]{1,0:T(8,128)} %bitcast.11, ...), custom_call_target="tpu_custom_call" | custom-call | tf_op jit(solution)/shard_map/step/pallas_call | solution.py:791
  124.4 130.5 %deliver.1 = (f32[1,1]{1,0:T(1,128)}, bf16[2048,512]{1,0:T(8,128)(2,1)}, bf16[2048,512]{1,0:T(8,128)(2,1)}, f32[512,512]{1,0:T(8,128)}, f32[512,256]{1,0:T(8,128)}) custom-call(f32[8,128]{1,0:T(8,128)} %get-tuple-element.14.loss, bf16[2048,512]{1,0:T(8,128)(2,1)} %get-tuple-element.15.grad_a, bf16[2048,512]{1,0:T(8,128)(2,1)} %get-tuple-element.16.grad_b, ...), custom_call_target="tpu_custom_call" | custom-call | tf_op jit(solution)/shard_map/deliver/pallas_call | solution.py:811

commit v5 on v4

--- a/solution.py
+++ b/solution.py
@@ -358,17 +358,29 @@
             peer(d),
         )
 
+    finish(0)
+
+    wait_both(neg_first)
+    start_both(neg_second)
     start_all(to_key, n_narrow)
     keys_in[rows_of(n, cap), :] = embed[1, rows_of(n, cap), :]
-
-    finish(0)
-
-    wait_both(neg_first)
-    start_both(neg_second)
 
     @pl.loop(0, blocks)
     def _(i):
         query[rows_of(i, block), :] = gather(dest_col, embed[0], i).astype(BF16)
+
+    wh_two[...] = jnp.zeros_like(wh_two)
+    wh_one[...] = jnp.zeros_like(wh_one)
+
+    def view_rows(v, rows):
+        return feat_slot[rows, :] if v else feat[0, rows, :]
+
+    for v in range(2):
+
+        @pl.loop(0, blocks)
+        def _(i):
+            rows = rows_of(i, block)
+            wh_two[v] += dot(view_rows(v, rows), normed[v, rows, :], TN)
 
     wait_both(neg_second)
     total_negs = n_narrow * neg_count
@@ -385,19 +397,6 @@
         power = power.astype(BF16)
         expo[rows, :] = power
         num[rows, :] = dot(power, table)
-
-    wh_two[...] = jnp.zeros_like(wh_two)
-    wh_one[...] = jnp.zeros_like(wh_one)
-
-    def view_rows(v, rows):
-        return feat_slot[rows, :] if v else feat[0, rows, :]
-
-    for v in range(2):
-
-        @pl.loop(0, blocks)
-        def _(i):
-            rows = rows_of(i, block)
-            wh_two[v] += dot(view_rows(v, rows), normed[v, rows, :], TN)
 
     loss_acc[...] = jnp.zeros_like(loss_acc)
 
@@ -671,17 +670,22 @@
     swap.wait()
 
 
-def deliver_kernel(loss, grad_a, grad_b, grads, loss_o, out_a, out_b, out_wh, out_wo, sems):
-    pieces = sems.shape[1]
+def deliver_kernel(
+    loss, grad_a, grad_b, grads, loss_o, out_a, out_b, out_wh, out_wo, held, read_sem, write_sem
+):
+    pieces = read_sem.shape[1]
     rows = grad_a.shape[0] // pieces
-    copies = [
-        pltpu.make_async_copy(
-            src.at[pl.ds(i * rows, rows)], dst.at[pl.ds(i * rows, rows)], sems.at[v, i]
-        )
-        for v, (src, dst) in enumerate(((grad_a, out_a), (grad_b, out_b)))
-        for i in range(pieces)
-    ]
-    for copy in copies:
+    reads, writes = [], []
+    for v, (src, dst) in enumerate(((grad_a, out_a), (grad_b, out_b))):
+        for i in range(pieces):
+            part = pl.ds(i * rows, rows)
+            middle = held.at[v, part]
+            reads.append(pltpu.make_async_copy(src.at[part], middle, read_sem.at[v, i]))
+            writes.append(pltpu.make_async_copy(middle, dst.at[part], write_sem.at[v, i]))
+    for copy in reads:
+        copy.start()
+    for arrived, copy in zip(reads, writes):
+        arrived.wait()
         copy.start()
     depth, hidden = out_wh.shape
     width = out_wo.shape[1]
@@ -689,9 +693,8 @@
         out_wh[:, p * width : (p + 1) * width] = grads[p * depth : (p + 1) * depth, :].astype(F32)
     out_wo[...] = grads[hidden // width * depth :, :].astype(F32)
     loss_o[...] = loss[0:1, 0:1]
-    for copy in copies:
+    for copy in writes:
         copy.wait()
-
 
 def body(feat_a, feat_b, w_hidden, w_out, send_rows, dest_rows, counts, neg_rows):
     points, depth = feat_a.shape[2:]
@@ -819,7 +822,7 @@
         ),
         in_specs=[vmem, anywhere, anywhere, vmem],
         out_specs=(vmem, anywhere, anywhere, vmem, vmem),
-        scratch_shapes=[dma((2, 4))],
+        scratch_shapes=[pltpu.VMEM((2, points, depth), BF16), dma((2, 4)), dma((2, 4))],
         compiler_params=pltpu.CompilerParams(vmem_limit_bytes=63 * 1024 * 1024),
         name="deliver",
     )(loss, grad_a, grad_b, grads)

time: 255 us -> 119 us (0.47)
  Pallas kernels: 254 us -> 118 us
    pallas_call x1, Pallas kernels: 131 us -> 5.86 us  [body(): pl.pallas_call(deliver_kernel, out_shape=(jax.ShapeDtypeStruct((1, 1), F3...]
    pallas_call x1, Pallas kernels: 124 us -> 112 us  [body(): pl.pallas_call(functools.partial(step_kernel, all_points), out_shape=out_...]
where the time goes in v5:
time: 119 us
  Pallas kernels  118 us (99%)
    pallas_call x1, Pallas kernels, body(): pl.pallas_call(functools.partial(step_kernel, all_points), out_shape=out_...  112 us
    pallas_call x1, Pallas kernels, body(): pl.pallas_call(deliver_kernel, out_shape=(jax.ShapeDtypeStruct((1, 1), F3...  5.86 us

profile of v5, /device:TPU:1, one launch (start us, length us, event | category | flops | bytes accessed | tf_op | source)
XLA Modules:
  0.0 118.9 jit_solution(6234996653745269321)
XLA Ops:
  0.6 112.4 %step.1 = (f32[8,128]{1,0:T(8,128)}, bf16[2048,512]{1,0:T(8,128)(2,1)}, bf16[2048,512]{1,0:T(8,128)(2,1)}, bf16[1536,256]{1,0:T(8,128)(2,1)}) custom-call(bf16[2048,512]{1,0:T(8,128)(2,1)} %bitcast.9, bf16[2048,512]{1,0:T(8,128)(2,1)} %bitcast.10, bf16[512,512]{1,0:T(8,128)(2,1)} %w_hidden.1, bf16[512,256]{1,0:T(8,128)(2,1)} %w_out.1, s32[16,128]{1,0:T(8,128)} %bitcast.11, ...), custom_call_target="tpu_custom_call" | custom-call | tf_op jit(solution)/shard_map/step/pallas_call | solution.py:794
  113.0 5.9 %deliver.1 = (f32[1,1]{1,0:T(1,128)}, bf16[2048,512]{1,0:T(8,128)(2,1)}, bf16[2048,512]{1,0:T(8,128)(2,1)}, f32[512,512]{1,0:T(8,128)}, f32[512,256]{1,0:T(8,128)}) custom-call(f32[8,128]{1,0:T(8,128)} %get-tuple-element.14.loss, bf16[2048,512]{1,0:T(8,128)(2,1)} %get-tuple-element.15.grad_a, bf16[2048,512]{1,0:T(8,128)(2,1)} %get-tuple-element.16.grad_b, ...), custom_call_target="tpu_custom_call" | custom-call | tf_op jit(solution)/shard_map/deliver/pallas_call | solution.py:814

commit v6 on v5

--- a/solution.py
+++ b/solution.py
@@ -43,20 +43,17 @@
 
 
 def start_all(make, count):
-    @pl.loop(1, count)
-    def _(d):
+    for d in range(1, count):
         make(d).start()
 
 
 def wait_all(make, count):
-    @pl.loop(1, count)
-    def _(d):
+    for d in range(1, count):
         make(d).wait()
 
 
 def wait_sent(make, count):
-    @pl.loop(1, count)
-    def _(d):
+    for d in range(1, count):
         make(d).wait_send()
 
 
@@ -127,6 +124,11 @@
     piece,
     chunk,
     stack_in,
+    half_wo,
+    own_wo,
+    piece_wo,
+    chunk_wo,
+    stack_wo,
     sem_in,
     sem_out,
     sem_msg,
@@ -157,6 +159,12 @@
     small = min(256, points)
     blocks = points // block
     split = hidden // 2
+    parts = hidden // width
+    wh_first, wo_first = 0, parts * depth
+    sets = (
+        (half, own, piece, chunk, stack_in),
+        (half_wo, own_wo, piece_wo, chunk_wo, stack_wo),
+    )
     side = negs.shape[0]
     upper = neg_count // 2
     row, col = n // side, lax.rem(n, side)
@@ -182,12 +190,9 @@
 
     barrier = pltpu.get_barrier_semaphore()
 
-    @pl.loop(1, n_narrow)
-    def _(d):
+    for d in range(1, n_narrow):
         pl.semaphore_signal(barrier, inc=1, device_id=peer(d), device_id_type=MESH)
-
-    @pl.loop(1, n_wide)
-    def _(d):
+    for d in range(1, n_wide):
         pl.semaphore_signal(barrier, inc=1, device_id=across(d), device_id_type=MESH)
 
     def load(v, i):
@@ -275,12 +280,16 @@
         start_all(to_msg, n_narrow)
         msg_in[n] = msg[n]
         columns(send_row[...], send_col)
-
-        @pl.loop(0, blocks)
+        to_slots(0, blocks - 1)
+
+    def to_slots(low, high):
+        @pl.loop(low, high)
         def _(i):
             feat_slot[rows_of(i, block), :] = gather(send_col, feat[1], i).astype(BF16)
 
     def slot_linear():
+        to_slots(blocks - 1, blocks)
+
         @pl.loop(0, blocks)
         def _(i):
             rows = rows_of(i, block)
@@ -554,6 +563,80 @@
 
     back_top(1, grad_b)
 
+    z, c = w // 2, lax.rem(w, 2)
+    partner = (2 * z + 1 - c, n)
+
+    def sum_stages(k, first):
+        half, own, piece, chunk, stack_in = sets[k]
+        span, rows = half.shape[0], chunk.shape[0]
+        mine = pl.multiple_of(first + c * span, 16)
+        other = pl.multiple_of(first + (1 - c) * span, 16)
+        place = pl.ds(pl.multiple_of(mine + n * rows, 16), rows)
+
+        def swap():
+            return remote(grads.at[pl.ds(other, span)], half, sem_pair.at[k], 0, partner)
+
+        def to_piece(d):
+            return remote(
+                own.at[rows_of(lax.rem(n + d, n_narrow), rows)],
+                piece.at[n],
+                sem_piece.at[k],
+                d,
+                peer(d),
+            )
+
+        def start_piece():
+            own[...] = (
+                grads[pl.ds(mine, span), :].astype(F32) + half[...].astype(F32)
+            ).astype(BF16)
+            start_all(to_piece, n_narrow)
+            piece[n] = own[rows_of(n, rows), :]
+
+        def to_stack(d):
+            return remote(
+                chunk,
+                stack_in.at[z],
+                sem_stack.at[k],
+                d,
+                (2 * lax.rem(z + d, n_z) + c, n),
+            )
+
+        def start_stack():
+            wait_all(to_piece, n_narrow)
+            chunk[...] = jnp.sum(piece[...].astype(F32), axis=0).astype(BF16)
+            start_all(to_stack, n_z)
+            stack_in[z] = chunk[...]
+
+        def to_gather(d):
+            return remote(grads_o.at[place], grads_o.at[place], sem_gather.at[k], d, peer(d))
+
+        def start_gather():
+            wait_all(to_stack, n_z)
+            grads_o[place, :] = jnp.sum(stack_in[...].astype(F32), axis=0).astype(BF16)
+            start_all(to_gather, n_narrow)
+
+        def last():
+            part = grads_o.at[pl.ds(mine, span)]
+            return remote(part, part, sem_pair.at[k], 1, partner)
+
+        def start_last():
+            wait_all(to_gather, n_narrow)
+            last().start()
+
+        def finish_last():
+            last().wait()
+
+        return swap, start_piece, start_stack, start_gather, start_last, finish_last
+
+    grads[wo_first:, :] = wo_acc[...].T.astype(BF16)
+    send_wo = sum_stages(1, wo_first)
+    send_wo[0]().start()
+
+    def wo_piece():
+        send_wo[0]().wait()
+        send_wo[1]()
+        first_product(1)
+
     put_sums(stat2, jnp.sum(acc[...], axis=1))
     stat2[0:1, split:] = loss_acc[0:1, :]
     stat2[1:8, split:] = jnp.broadcast_to(
@@ -567,16 +650,17 @@
         total2,
         sem_near2,
         sem_far2,
-        lambda: first_product(1),
+        wo_piece,
+        send_wo[2],
     )
 
     pair_total = total2[1:2, split : split + 1]
     grad_weight = all_points / pair_total
-    loss_o[...] = jnp.broadcast_to(total2[0:1, split:] / pair_total, loss_o.shape)
+    loss_o[0:1, :] = total2[0:1, split:] / pair_total
     mean_grads = [get_sum(total2, 2 * v) * inv_count for v in range(2)]
     mean_crosses = [get_sum(total2, 2 * v + 1) * inv_count for v in range(2)]
     scales = [inverses[v] * grad_weight for v in range(2)]
-    parts = hidden // width
+    loss_o[1:2, :] = jnp.broadcast_to(grad_weight, (1, cap))
     totals = [jnp.sum(feat_acc[v], axis=0, keepdims=True) for v in range(2)]
     downs = [jnp.broadcast_to(row, (8, depth)).T[:, 0:1] for row in totals]
     for p in range(parts):
@@ -591,7 +675,6 @@
             for v in range(2)
         )
         grads[p * depth : (p + 1) * depth, :] = value.astype(BF16)
-    grads[parts * depth :, :] = (wo_acc[...].T * grad_weight).astype(BF16)
 
     def store(v, i):
         ref = (grad_feat_a, grad_feat_b)[v]
@@ -619,55 +702,24 @@
             normed[1, rows_of(i, block), :] = dot(picks, feat_slot[...]).astype(BF16)
             store(1, i).start()
 
-    span, rows = half.shape[0], chunk.shape[0]
-    z, c = w // 2, lax.rem(w, 2)
-    partner = (2 * z + 1 - c, n)
-    mine = pl.multiple_of(c * span, span)
-    other = pl.multiple_of((1 - c) * span, span)
-    swap = remote(grads.at[pl.ds(other, span)], half, sem_pair, 0, partner)
+    send_wh = sum_stages(0, wh_first)
+    swap = send_wh[0]()
     swap.start()
     swap.wait()
-    own[...] = (
-        grads[pl.ds(mine, span), :].astype(F32) + half[...].astype(F32)
-    ).astype(BF16)
-
-    def to_piece(d):
-        return remote(
-            own.at[rows_of(lax.rem(n + d, n_narrow), rows)], piece.at[n], sem_piece, d, peer(d)
-        )
-
-    start_all(to_piece, n_narrow)
-    piece[n] = own[rows_of(n, rows), :]
+    send_wh[1]()
     feat_grad(0)
-    wait_all(to_piece, n_narrow)
-    chunk[...] = jnp.sum(piece[...].astype(F32), axis=0).astype(BF16)
-
-    def to_stack(d):
-        return remote(
-            chunk, stack_in.at[z], sem_stack, d, (2 * lax.rem(z + d, n_z) + c, n)
-        )
-
-    start_all(to_stack, n_z)
-    stack_in[z] = chunk[...]
+    send_wh[2]()
     feat_grad(1)
-    wait_all(to_stack, n_z)
-    place = pl.ds(pl.multiple_of(mine + n * rows, rows), rows)
-    grads_o[place, :] = jnp.sum(stack_in[...].astype(F32), axis=0).astype(BF16)
-
-    def to_gather(d):
-        return remote(grads_o.at[place], grads_o.at[place], sem_gather, d, peer(d))
-
-    start_all(to_gather, n_narrow)
+    send_wo[3]()
+    send_wh[3]()
     row_order()
-    wait_all(to_gather, n_narrow)
-    swap = remote(
-        grads_o.at[pl.ds(mine, span)], grads_o.at[pl.ds(mine, span)], sem_pair, 1, partner
-    )
-    swap.start()
+    send_wo[4]()
+    send_wh[4]()
     for v in range(2):
         for i in range(blocks):
             store(v, i).wait()
-    swap.wait()
+    send_wo[5]()
+    send_wh[5]()
 
 
 def deliver_kernel(
@@ -691,7 +743,7 @@
     width = out_wo.shape[1]
     for p in range(hidden // width):
         out_wh[:, p * width : (p + 1) * width] = grads[p * depth : (p + 1) * depth, :].astype(F32)
-    out_wo[...] = grads[hidden // width * depth :, :].astype(F32)
+    out_wo[...] = grads[hidden // width * depth :, :].astype(F32) * loss[1:2, 0:1]
     loss_o[...] = loss[0:1, 0:1]
     for copy in writes:
         copy.wait()
@@ -710,8 +762,19 @@
     stat = (8, hidden // 2)
     stat2 = (8, hidden // 2 + cap)
     grad_total = depth * hidden // width + hidden
-    span = grad_total // 2
-    rows = span // n_narrow
+    wh_rows = depth * hidden // width
+
+    def sum_scratch(total):
+        span = total // 2
+        rows = span // n_narrow
+        return (
+            pltpu.VMEM((span, width), BF16),
+            pltpu.VMEM((span, width), BF16),
+            pltpu.VMEM((n_narrow, rows, width), BF16),
+            pltpu.VMEM((rows, width), BF16),
+            pltpu.VMEM((n_z, rows, width), BF16),
+        )
+
     vmem = pl.BlockSpec(memory_space=pltpu.VMEM)
     anywhere = pl.BlockSpec(memory_space=pl.ANY)
     dma = pltpu.SemaphoreType.DMA
@@ -770,11 +833,8 @@
         pltpu.VMEM((2, depth, hidden), F32),
         pltpu.VMEM((8, cap), F32),
         pltpu.VMEM((grad_total, width), BF16),
-        pltpu.VMEM((span, width), BF16),
-        pltpu.VMEM((span, width), BF16),
-        pltpu.VMEM((n_narrow, rows, width), BF16),
-        pltpu.VMEM((rows, width), BF16),
-        pltpu.VMEM((n_z, rows, width), BF16),
+        *sum_scratch(wh_rows),
+        *sum_scratch(hidden),
         dma((2, blocks)),
         dma((2, blocks)),
         dma((2, n_narrow)),
@@ -786,10 +846,10 @@
         dma((2, n_narrow)),
         dma((2, n_narrow)),
         dma((2, 4 * side)),
-        dma((2, 2)),
-        dma((2, n_narrow)),
-        dma((2, n_z)),
-        dma((2, n_narrow)),
+        dma((2, 2, 2)),
+        dma((2, 2, n_narrow)),
+        dma((2, 2, n_z)),
+        dma((2, 2, n_narrow)),
     ]
     loss, grad_a, grad_b, grads = pl.pallas_call(
         functools.partial(step_kernel, all_points),

time: 119 us -> 116 us (0.975)
  Pallas kernels: 118 us -> 115 us
    pallas_call x1, Pallas kernels: 112 us -> 109 us  [body(): pl.pallas_call(functools.partial(step_kernel, all_points), out_shape=out_...]
where the time goes in v6:
time: 116 us
  Pallas kernels  115 us (99%)
    pallas_call x1, Pallas kernels, body(): pl.pallas_call(functools.partial(step_kernel, all_points), out_shape=out_...  109 us
    pallas_call x1, Pallas kernels, body(): pl.pallas_call(deliver_kernel, out_shape=(jax.ShapeDtypeStruct((1, 1), F3...  5.86 us

profile of v6, /device:TPU:1, one launch (start us, length us, event | category | flops | bytes accessed | tf_op | source)
XLA Modules:
  0.0 116.0 jit_solution(1877471812356928250)
XLA Ops:
  0.6 109.4 %step.1 = (f32[8,128]{1,0:T(8,128)}, bf16[2048,512]{1,0:T(8,128)(2,1)}, bf16[2048,512]{1,0:T(8,128)(2,1)}, bf16[1536,256]{1,0:T(8,128)(2,1)}) custom-call(bf16[2048,512]{1,0:T(8,128)(2,1)} %bitcast.9, bf16[2048,512]{1,0:T(8,128)(2,1)} %bitcast.10, bf16[512,512]{1,0:T(8,128)(2,1)} %w_hidden.1, bf16[512,256]{1,0:T(8,128)(2,1)} %w_out.1, s32[16,128]{1,0:T(8,128)} %bitcast.11, ...), custom_call_target="tpu_custom_call" | custom-call | tf_op jit(solution)/shard_map/step/pallas_call | solution.py:854
  110.0 5.9 %deliver.1 = (f32[1,1]{1,0:T(1,128)}, bf16[2048,512]{1,0:T(8,128)(2,1)}, bf16[2048,512]{1,0:T(8,128)(2,1)}, f32[512,512]{1,0:T(8,128)}, f32[512,256]{1,0:T(8,128)}) custom-call(f32[8,128]{1,0:T(8,128)} %get-tuple-element.14.loss, bf16[2048,512]{1,0:T(8,128)(2,1)} %get-tuple-element.15.grad_a, bf16[2048,512]{1,0:T(8,128)(2,1)} %get-tuple-element.16.grad_b, ...), custom_call_target="tpu_custom_call" | custom-call | tf_op jit(solution)/shard_map/deliver/pallas_call | solution.py:874

commit v7 on v6

--- a/solution.py
+++ b/solution.py
@@ -61,6 +61,16 @@
     all_points,
     feat_a,
     feat_b,
+    w_hidden_in,
+    w_out_in,
+    send_in,
+    dest_in,
+    counts_in,
+    neg_in,
+    loss_out,
+    grad_feat_a,
+    grad_feat_b,
+    grads_out,
     w_hidden,
     w_out,
     send_row,
@@ -68,8 +78,6 @@
     counts,
     neg_row,
     loss_o,
-    grad_feat_a,
-    grad_feat_b,
     grads_o,
     feat,
     feat_slot,
@@ -129,6 +137,8 @@
     piece_wo,
     chunk_wo,
     stack_wo,
+    sem_small,
+    sem_result,
     sem_in,
     sem_out,
     sem_msg,
@@ -195,6 +205,21 @@
     for d in range(1, n_wide):
         pl.semaphore_signal(barrier, inc=1, device_id=across(d), device_id_type=MESH)
 
+    small_loads = [
+        pltpu.make_async_copy(src, dst, sem_small.at[k])
+        for k, (src, dst) in enumerate(
+            (
+                (w_hidden_in, w_hidden),
+                (w_out_in, w_out),
+                (send_in, send_row),
+                (dest_in, dest_own),
+                (counts_in, counts),
+                (neg_in, neg_row),
+            )
+        )
+    ]
+    small_loads[0].start()
+
     def load(v, i):
         ref = (feat_a, feat_b)[v]
         rows = rows_of(i, block)
@@ -203,6 +228,9 @@
     for v in (1, 0):
         for i in range(blocks):
             load(v, i).start()
+    for copy in small_loads[1:]:
+        copy.start()
+    small_loads[0].wait()
 
     acc[...] = jnp.zeros_like(acc)
     feat_acc[...] = jnp.zeros_like(feat_acc)
@@ -228,6 +256,8 @@
             [total[2 * r : 2 * r + 1, 0:split], total[2 * r + 1 : 2 * r + 2, 0:split]], axis=1
         )
 
+    for copy in small_loads[1:]:
+        copy.wait()
     put_sums(stat, jnp.sum(acc[...], axis=1))
 
     pl.semaphore_wait(barrier, n_narrow + n_wide - 2)
@@ -619,14 +649,26 @@
             part = grads_o.at[pl.ds(mine, span)]
             return remote(part, part, sem_pair.at[k], 1, partner)
 
+        def write(k2, first):
+            part = pl.ds(first, span)
+            return pltpu.make_async_copy(
+                grads_o.at[part], grads_out.at[part], sem_result.at[2 * k + k2]
+            )
+
         def start_last():
             wait_all(to_gather, n_narrow)
             last().start()
+            write(0, mine).start()
 
         def finish_last():
             last().wait()
-
-        return swap, start_piece, start_stack, start_gather, start_last, finish_last
+            write(1, other).start()
+
+        def end():
+            write(0, mine).wait()
+            write(1, other).wait()
+
+        return swap, start_piece, start_stack, start_gather, start_last, finish_last, end
 
     grads[wo_first:, :] = wo_acc[...].T.astype(BF16)
     send_wo = sum_stages(1, wo_first)
@@ -660,7 +702,9 @@
     mean_grads = [get_sum(total2, 2 * v) * inv_count for v in range(2)]
     mean_crosses = [get_sum(total2, 2 * v + 1) * inv_count for v in range(2)]
     scales = [inverses[v] * grad_weight for v in range(2)]
-    loss_o[1:2, :] = jnp.broadcast_to(grad_weight, (1, cap))
+    loss_o[1:8, :] = jnp.broadcast_to(grad_weight, (7, cap))
+    loss_write = pltpu.make_async_copy(loss_o, loss_out, sem_result.at[4])
+    loss_write.start()
     totals = [jnp.sum(feat_acc[v], axis=0, keepdims=True) for v in range(2)]
     downs = [jnp.broadcast_to(row, (8, depth)).T[:, 0:1] for row in totals]
     for p in range(parts):
@@ -715,15 +759,34 @@
     row_order()
     send_wo[4]()
     send_wh[4]()
+    send_wo[5]()
+    send_wh[5]()
     for v in range(2):
         for i in range(blocks):
             store(v, i).wait()
-    send_wo[5]()
-    send_wh[5]()
+    send_wo[6]()
+    send_wh[6]()
+    loss_write.wait()
 
 
 def deliver_kernel(
-    loss, grad_a, grad_b, grads, loss_o, out_a, out_b, out_wh, out_wo, held, read_sem, write_sem
+    loss_in,
+    grad_a,
+    grad_b,
+    grads_in,
+    loss_o,
+    out_a,
+    out_b,
+    out_wh,
+    out_wo,
+    loss,
+    grads,
+    wh,
+    wo,
+    held,
+    sem,
+    read_sem,
+    write_sem,
 ):
     pieces = read_sem.shape[1]
     rows = grad_a.shape[0] // pieces
@@ -734,16 +797,26 @@
             middle = held.at[v, part]
             reads.append(pltpu.make_async_copy(src.at[part], middle, read_sem.at[v, i]))
             writes.append(pltpu.make_async_copy(middle, dst.at[part], write_sem.at[v, i]))
-    for copy in reads:
+    first = [
+        pltpu.make_async_copy(grads_in, grads, sem.at[0]),
+        pltpu.make_async_copy(loss_in, loss, sem.at[1]),
+    ]
+    for copy in first + reads:
         copy.start()
+    for copy in first:
+        copy.wait()
+    depth, hidden = wh.shape
+    width = wo.shape[1]
+    for p in range(hidden // width):
+        wh[:, p * width : (p + 1) * width] = grads[p * depth : (p + 1) * depth, :].astype(F32)
+    writes.append(pltpu.make_async_copy(wh, out_wh, sem.at[2]))
+    writes[-1].start()
+    wo[...] = grads[hidden // width * depth :, :].astype(F32) * loss[1:2, 0:1]
+    writes.append(pltpu.make_async_copy(wo, out_wo, sem.at[3]))
+    writes[-1].start()
     for arrived, copy in zip(reads, writes):
         arrived.wait()
         copy.start()
-    depth, hidden = out_wh.shape
-    width = out_wo.shape[1]
-    for p in range(hidden // width):
-        out_wh[:, p * width : (p + 1) * width] = grads[p * depth : (p + 1) * depth, :].astype(F32)
-    out_wo[...] = grads[hidden // width * depth :, :].astype(F32) * loss[1:2, 0:1]
     loss_o[...] = loss[0:1, 0:1]
     for copy in writes:
         copy.wait()
@@ -785,6 +858,14 @@
         jax.ShapeDtypeStruct((grad_total, width), BF16),
     )
     scratch = [
+        pltpu.VMEM((depth, hidden), BF16),
+        pltpu.VMEM((hidden, width), BF16),
+        pltpu.VMEM((n_narrow, cap), jnp.int32),
+        pltpu.VMEM((n_narrow, cap), jnp.int32),
+        pltpu.VMEM((1, n_narrow), jnp.int32),
+        pltpu.VMEM((1, neg_count), jnp.int32),
+        pltpu.VMEM((8, cap), F32),
+        pltpu.VMEM((grad_total, width), BF16),
         pltpu.VMEM((2, points, depth), BF16),
         pltpu.VMEM((points, depth), BF16),
         pltpu.VMEM((points, hidden), F32),
@@ -835,6 +916,8 @@
         pltpu.VMEM((grad_total, width), BF16),
         *sum_scratch(wh_rows),
         *sum_scratch(hidden),
+        dma((6,)),
+        dma((5,)),
         dma((2, blocks)),
         dma((2, blocks)),
         dma((2, n_narrow)),
@@ -854,8 +937,8 @@
     loss, grad_a, grad_b, grads = pl.pallas_call(
         functools.partial(step_kernel, all_points),
         out_shape=out_shape,
-        in_specs=[anywhere] * 2 + [vmem] * 6,
-        out_specs=(vmem, anywhere, anywhere, vmem),
+        in_specs=[anywhere] * 8,
+        out_specs=(anywhere,) * 4,
         scratch_shapes=scratch,
         compiler_params=pltpu.CompilerParams(
             collective_id=1, has_side_effects=True, vmem_limit_bytes=63 * 1024 * 1024
@@ -880,9 +963,18 @@
             jax.ShapeDtypeStruct((depth, hidden), F32),
             jax.ShapeDtypeStruct((hidden, width), F32),
         ),
-        in_specs=[vmem, anywhere, anywhere, vmem],
-        out_specs=(vmem, anywhere, anywhere, vmem, vmem),
-        scratch_shapes=[pltpu.VMEM((2, points, depth), BF16), dma((2, 4)), dma((2, 4))],
+        in_specs=[anywhere] * 4,
+        out_specs=(vmem,) + (anywhere,) * 4,
+        scratch_shapes=[
+            pltpu.VMEM((8, cap), F32),
+            pltpu.VMEM((grad_total, width), BF16),
+            pltpu.VMEM((depth, hidden), F32),
+            pltpu.VMEM((hidden, width), F32),
+            pltpu.VMEM((2, points, depth), BF16),
+            dma((4,)),
+            dma((2, 4)),
+            dma((2, 4)),
+        ],
         compiler_params=pltpu.CompilerParams(vmem_limit_bytes=63 * 1024 * 1024),
         name="deliver",
     )(loss, grad_a, grad_b, grads)

time: 116 us -> 115 us (level)
  no operation moved by 1% of the time
where the time goes in v7:
time: 115 us
  Pallas kernels  114 us (99%)
    pallas_call x1, Pallas kernels, body(): pl.pallas_call(functools.partial(step_kernel, all_points), out_shape=out_...  109 us
    pallas_call x1, Pallas kernels, body(): pl.pallas_call(deliver_kernel, out_shape=(jax.ShapeDtypeStruct((1, 1), F3...  5.37 us

profile of v7, /device:TPU:1, one launch (start us, length us, event | category | flops | bytes accessed | tf_op | source)
XLA Modules:
  0.0 114.8 jit_solution(9586141498024603178)
XLA Ops:
  0.6 108.6 %step.1 = (f32[8,128]{1,0:T(8,128)}, bf16[2048,512]{1,0:T(8,128)(2,1)}, bf16[2048,512]{1,0:T(8,128)(2,1)}, bf16[1536,256]{1,0:T(8,128)(2,1)}) custom-call(bf16[2048,512]{1,0:T(8,128)(2,1)} %bitcast.9, bf16[2048,512]{1,0:T(8,128)(2,1)} %bitcast.10, bf16[512,512]{1,0:T(8,128)(2,1)} %w_hidden_in.1, bf16[512,256]{1,0:T(8,128)(2,1)} %w_out_in.1, ...), custom_call_target="tpu_custom_call" | custom-call | tf_op jit(solution)/shard_map/step/pallas_call | solution.py:937
  109.3 5.4 %deliver.1 = (f32[1,1]{1,0:T(1,128)}, bf16[2048,512]{1,0:T(8,128)(2,1)}, bf16[2048,512]{1,0:T(8,128)(2,1)}, f32[512,512]{1,0:T(8,128)}, f32[512,256]{1,0:T(8,128)}) custom-call(f32[8,128]{1,0:T(8,128)} %get-tuple-element.14.loss_in, bf16[2048,512]{1,0:T(8,128)(2,1)} %get-tuple-element.15.grad_a, bf16[2048,512]{1,0:T(8,128)(2,1)} %get-tuple-element.16.grad_b, ...), custom_call_target="tpu_custom_call" | custom-call | tf_op jit(solution)/shard_map/deliver/pallas_call | solution.py:957

commit v8 on v7

--- a/solution.py
+++ b/solution.py
@@ -42,8 +42,8 @@
     )
 
 
-def start_all(make, count):
-    for d in range(1, count):
+def start_all(make, count, order=None):
+    for d in order or range(1, count):
         make(d).start()
 
 
@@ -180,8 +180,22 @@
     row, col = n // side, lax.rem(n, side)
     halves = (slice(0, upper), slice(upper, neg_count))
 
+    def steps(d):
+        if isinstance(d, int):
+            return d // side, d % side
+        return lax.div(d, side), lax.rem(d, side)
+
+    def hops(d):
+        return sum(min(k, side - k) for k in steps(d))
+
+    far_first = sorted(range(1, n_narrow), key=hops, reverse=True)
+
+    def target(d):
+        down, right = steps(d)
+        return lax.rem(row + down, side) * side + lax.rem(col + right, side)
+
     def peer(d):
-        return (w, lax.rem(n + d, n_narrow))
+        return (w, target(d))
 
     def along_row(d):
         return (w, row * side + lax.rem(col + d, side))
@@ -190,7 +204,8 @@
         return (w, lax.rem(row + d, side) * side + col)
 
     def source(d):
-        return lax.rem(n + n_narrow - d, n_narrow)
+        down, right = steps(d)
+        return lax.rem(row + side - down, side) * side + lax.rem(col + side - right, side)
 
     def across(d):
         return (lax.rem(w + d, n_wide), n)
@@ -269,7 +284,7 @@
         def to_far(d):
             return remote(part, far.at[w], sem_far, d, across(d))
 
-        start_all(to_near, n_narrow)
+        start_all(to_near, n_narrow, far_first)
         near[n] = stat[...]
         if between is not None:
             between()
@@ -283,7 +298,7 @@
         total[...] = jnp.sum(far[...], axis=0)
 
     def to_msg(d):
-        return remote(msg.at[lax.rem(n + d, n_narrow)], msg_in.at[n], sem_msg, d, peer(d))
+        return remote(msg.at[target(d)], msg_in.at[n], sem_msg, d, peer(d))
 
     def gather(ids, table, i):
         lanes = lax.broadcasted_iota(jnp.int32, (block, points), 1)
@@ -307,7 +322,7 @@
         line = lax.broadcasted_iota(jnp.int32, (8, cap), 0)
         for s in range(n_narrow):
             msg[s] = jnp.where(line == 0, dest_own[s : s + 1, :], count[s : s + 1, :])
-        start_all(to_msg, n_narrow)
+        start_all(to_msg, n_narrow, far_first)
         msg_in[n] = msg[n]
         columns(send_row[...], send_col)
         to_slots(0, blocks - 1)
@@ -390,7 +405,7 @@
 
     def to_key(d):
         return remote(
-            embed.at[1, rows_of(lax.rem(n + d, n_narrow), cap)],
+            embed.at[1, rows_of(target(d), cap)],
             keys_in.at[rows_of(n, cap)],
             sem_key,
             d,
@@ -401,7 +416,7 @@
 
     wait_both(neg_first)
     start_both(neg_second)
-    start_all(to_key, n_narrow)
+    start_all(to_key, n_narrow, far_first)
     keys_in[rows_of(n, cap), :] = embed[1, rows_of(n, cap), :]
 
     @pl.loop(0, blocks)
@@ -608,7 +623,7 @@
 
         def to_piece(d):
             return remote(
-                own.at[rows_of(lax.rem(n + d, n_narrow), rows)],
+                own.at[rows_of(target(d), rows)],
                 piece.at[n],
                 sem_piece.at[k],
                 d,
@@ -619,7 +634,7 @@
             own[...] = (
                 grads[pl.ds(mine, span), :].astype(F32) + half[...].astype(F32)
             ).astype(BF16)
-            start_all(to_piece, n_narrow)
+            start_all(to_piece, n_narrow, far_first)
             piece[n] = own[rows_of(n, rows), :]
 
         def to_stack(d):
@@ -643,7 +658,7 @@
         def start_gather():
             wait_all(to_stack, n_z)
             grads_o[place, :] = jnp.sum(stack_in[...].astype(F32), axis=0).astype(BF16)
-            start_all(to_gather, n_narrow)
+            start_all(to_gather, n_narrow, far_first)
 
         def last():
             part = grads_o.at[pl.ds(mine, span)]

time: 115 us -> 113 us (0.983)
  Pallas kernels: 114 us -> 112 us
    pallas_call x1, Pallas kernels: 109 us -> 107 us  [body(): pl.pallas_call(functools.partial(step_kernel, all_points), out_shape=out_...]
where the time goes in v8:
time: 113 us
  Pallas kernels  112 us (99%)
    pallas_call x1, Pallas kernels, body(): pl.pallas_call(functools.partial(step_kernel, all_points), out_shape=out_...  107 us
    pallas_call x1, Pallas kernels, body(): pl.pallas_call(deliver_kernel, out_shape=(jax.ShapeDtypeStruct((1, 1), F3...  5.37 us

profile of v8, /device:TPU:1, one launch (start us, length us, event | category | flops | bytes accessed | tf_op | source)
XLA Modules:
  0.0 112.7 jit_solution(2613838449686268655)
XLA Ops:
  0.6 106.5 %step.1 = (f32[8,128]{1,0:T(8,128)}, bf16[2048,512]{1,0:T(8,128)(2,1)}, bf16[2048,512]{1,0:T(8,128)(2,1)}, bf16[1536,256]{1,0:T(8,128)(2,1)}) custom-call(bf16[2048,512]{1,0:T(8,128)(2,1)} %bitcast.9, bf16[2048,512]{1,0:T(8,128)(2,1)} %bitcast.10, bf16[512,512]{1,0:T(8,128)(2,1)} %w_hidden_in.1, bf16[512,256]{1,0:T(8,128)(2,1)} %w_out_in.1, ...), custom_call_target="tpu_custom_call" | custom-call | tf_op jit(solution)/shard_map/step/pallas_call | solution.py:952
  107.2 5.4 %deliver.1 = (f32[1,1]{1,0:T(1,128)}, bf16[2048,512]{1,0:T(8,128)(2,1)}, bf16[2048,512]{1,0:T(8,128)(2,1)}, f32[512,512]{1,0:T(8,128)}, f32[512,256]{1,0:T(8,128)}) custom-call(f32[8,128]{1,0:T(8,128)} %get-tuple-element.14.loss_in, bf16[2048,512]{1,0:T(8,128)(2,1)} %get-tuple-element.15.grad_a, bf16[2048,512]{1,0:T(8,128)(2,1)} %get-tuple-element.16.grad_b, ...), custom_call_target="tpu_custom_call" | custom-call | tf_op jit(solution)/shard_map/deliver/pallas_call | solution.py:972

commit v9 on v8

--- a/solution.py
+++ b/solution.py
@@ -481,7 +481,7 @@
         spread[:, rows] = (share * asked).T.astype(BF16)
         return jnp.sum(term, axis=0, keepdims=True)
 
-    pair = 2
+    pair = min(4, n_narrow)
 
     @pl.loop(0, n_narrow // pair)
     def _(i):

time: 113 us -> 113 us (level)
  no operation moved by 1% of the time
where the time goes in v9:
time: 113 us; the launch traced here: 112 us
  Pallas kernels  112 us (99%)
    pallas_call x1, Pallas kernels, body(): pl.pallas_call(functools.partial(step_kernel, all_points), out_shape=out_...  106 us
    pallas_call x1, Pallas kernels, body(): pl.pallas_call(deliver_kernel, out_shape=(jax.ShapeDtypeStruct((1, 1), F3...  5.37 us

profile of v9, /device:TPU:1, one launch (start us, length us, event | category | flops | bytes accessed | tf_op | source)
XLA Modules:
  0.0 112.4 jit_solution(6636696777429213564)
XLA Ops:
  0.6 106.3 %step.1 = (f32[8,128]{1,0:T(8,128)}, bf16[2048,512]{1,0:T(8,128)(2,1)}, bf16[2048,512]{1,0:T(8,128)(2,1)}, bf16[1536,256]{1,0:T(8,128)(2,1)}) custom-call(bf16[2048,512]{1,0:T(8,128)(2,1)} %bitcast.9, bf16[2048,512]{1,0:T(8,128)(2,1)} %bitcast.10, bf16[512,512]{1,0:T(8,128)(2,1)} %w_hidden_in.1, bf16[512,256]{1,0:T(8,128)(2,1)} %w_out_in.1, ...), custom_call_target="tpu_custom_call" | custom-call | tf_op jit(solution)/shard_map/step/pallas_call | solution.py:952
  106.9 5.4 %deliver.1 = (f32[1,1]{1,0:T(1,128)}, bf16[2048,512]{1,0:T(8,128)(2,1)}, bf16[2048,512]{1,0:T(8,128)(2,1)}, f32[512,512]{1,0:T(8,128)}, f32[512,256]{1,0:T(8,128)}) custom-call(f32[8,128]{1,0:T(8,128)} %get-tuple-element.14.loss_in, bf16[2048,512]{1,0:T(8,128)(2,1)} %get-tuple-element.15.grad_a, bf16[2048,512]{1,0:T(8,128)(2,1)} %get-tuple-element.16.grad_b, ...), custom_call_target="tpu_custom_call" | custom-call | tf_op jit(solution)/shard_map/deliver/pallas_call | solution.py:972
